TPU v7x, 32 devices: a whole 2x2x4 slice. The times are simulated.
32 devices in a mesh: rep: 4 (over x, core), shard: 8 (over z, y).
Axes of the slice: x: 2, y: 2, z: 4, core: 2. Of those that a mesh axis runs over, the one named last changes fastest.
Arguments:
- tokens: bfloat16 [8, 2048, 896], P('rep', 'shard'), may hold values from -6 to 6
- segments: int32 [8, 2048], P('rep', 'shard'), may hold values from 0 to 2, as said below
- first_gain: bfloat16 [896], P('shard'), may hold values from 0.5 to 1.5
- query_weight: bfloat16 [896, 896], P('shard'), may hold values from -0.1875 to 0.1875
- query_bias: bfloat16 [896], P('shard'), may hold values from -3 to 3
- key_weight: bfloat16 [896, 128], P('shard'), may hold values from -0.1875 to 0.1875
- key_bias: bfloat16 [128], P('shard'), may hold values from -3 to 3
- value_weight: bfloat16 [896, 128], P('shard'), may hold values from -0.1875 to 0.1875
- value_bias: bfloat16 [128], P('shard'), may hold values from -3 to 3
- out_weight: bfloat16 [896, 896], P('shard'), may hold values from -0.75 to 0.75
- second_gain: bfloat16 [896], P('shard'), may hold values from 0.5 to 1.5
- gate_weight: bfloat16 [896, 4864], P('shard'), may hold values from -0.1875 to 0.1875
- up_weight: bfloat16 [896, 4864], P('shard'), may hold values from -0.1875 to 0.1875
- down_weight: bfloat16 [4864, 896], P('shard'), may hold values from -0.125 to 0.125
- cotangent: bfloat16 [8, 2048, 896], P('rep', 'shard'), may hold values from -6 to 6
Outputs:
- output: bfloat16 [8, 2048, 896], P('rep', 'shard')
- tokens_grad: bfloat16 [8, 2048, 896], P('rep', 'shard')
- first_gain_grad: float32 [896], P('shard')
- query_weight_grad: float32 [896, 896], P('shard')
- query_bias_grad: float32 [896], P('shard')
- key_weight_grad: float32 [896, 128], P('shard')
- key_bias_grad: float32 [128], P('shard')
- value_weight_grad: float32 [896, 128], P('shard')
- value_bias_grad: float32 [128], P('shard')
- out_weight_grad: float32 [896, 896], P('shard')
- second_gain_grad: float32 [896], P('shard')
- gate_weight_grad: float32 [896, 4864], P('shard')
- up_weight_grad: float32 [896, 4864], P('shard')
- down_weight_grad: float32 [4864, 896], P('shard')
Inputs may be any that keep to these rules, and one draw needn't show every extreme that they name: `segments`: along each sequence the segment numbers start at 0 and never fall.
All inputs are finite; a program needn't handle non-finite values.
Results may differ from a plain program's by a relative error of at most 0.033.
Values may be sent and summed in bfloat16 or wider, within the bound.
A program may use at most 320 MiB of HBM per device.

v0:
```python
import math

import jax
import jax.numpy as jnp
from jax import lax
from jax.sharding import PartitionSpec as P

HD = 64


EPSILON = 1e-06
THETA = 1000000.0
MASKED = -1000000000.0


def rms_scale(values):
    return lax.rsqrt(jnp.mean(values * values, axis=-1, keepdims=True) + EPSILON)


def rotate(values, cosine, sine_table):
    half_size = values.shape[-1] // 2
    first_half = values[..., :half_size]
    second_half = values[..., half_size:]
    cosine = cosine[:, None, :]
    sine_table = sine_table[:, None, :]
    return jnp.concatenate(
        [
            first_half * cosine - second_half * sine_table,
            second_half * cosine + first_half * sine_table,
        ],
        axis=-1,
    )


def inner_rows(left_side, right_side):
    return lax.dot_general(
        left_side, right_side, (((0,), (0,)), ((), ())), preferred_element_type=jnp.float32
    )


def times_transposed(left_side, right_side):
    return lax.dot_general(
        left_side, right_side, (((1,), (1,)), ((), ())), preferred_element_type=jnp.float32
    )


def norm_back(grad_normed, values, scale_rows, gain_value):
    normal = values * scale_rows
    grad_scaled = grad_normed * gain_value.astype(jnp.float32)
    return scale_rows * (
        grad_scaled - normal * jnp.mean(grad_scaled * normal, axis=-1, keepdims=True)
    )


def masked_scores(query_block, key_block, mask_block):
    raw_scores = jnp.einsum(
        "bqkgd,bskd->bkgqs", query_block, key_block, preferred_element_type=jnp.float32
    ) * HD ** (-0.5)
    return jnp.where(mask_block[:, None, None], raw_scores, MASKED)


def attend(items):
    query_block, key_block, value_block, mask_block = items
    scores = masked_scores(query_block, key_block, mask_block)
    row_max = jnp.max(scores, axis=-1, keepdims=True)
    weights = jnp.exp(scores - row_max)
    row_total = jnp.sum(weights, axis=-1, keepdims=True)
    probs = (weights / row_total).astype(jnp.bfloat16)
    mixed = jnp.einsum("bkgqs,bskd->bqkgd", probs, value_block, preferred_element_type=jnp.float32)
    return (mixed.astype(jnp.bfloat16), row_max + jnp.log(row_total))


def attend_back(items):
    query_block, key_block, value_block, mask_block, log_block, grad_block = items
    scores = masked_scores(query_block, key_block, mask_block)
    probs_full = jnp.exp(scores - log_block)
    grad_probs = jnp.einsum(
        "bqkgd,bskd->bkgqs", grad_block, value_block, preferred_element_type=jnp.float32
    )
    row_delta = jnp.sum(probs_full * grad_probs, axis=-1, keepdims=True)
    grad_scores = (probs_full * (grad_probs - row_delta)).astype(jnp.bfloat16)
    grad_query = jnp.einsum(
        "bkgqs,bskd->bqkgd", grad_scores, key_block, preferred_element_type=jnp.float32
    ) * HD ** (-0.5)
    grad_key = jnp.einsum(
        "bkgqs,bqkgd->bskd", grad_scores, query_block, preferred_element_type=jnp.float32
    ) * HD ** (-0.5)
    grad_value = jnp.einsum(
        "bkgqs,bqkgd->bskd",
        probs_full.astype(jnp.bfloat16),
        grad_block,
        preferred_element_type=jnp.float32,
    )
    return (grad_query, grad_key, grad_value)


def on_device(
    tokens,
    segments,
    first_gain,
    query_weight,
    query_bias,
    key_weight,
    key_bias,
    value_weight,
    value_bias,
    out_weight,
    second_gain,
    gate_weight,
    up_weight,
    down_weight,
    cotangent,
):
    sequences, local_tokens, model_width = tokens.shape
    row_count = sequences * local_tokens
    gathered = (
        lax.all_gather(first_gain, "shard", axis=0, tiled=True),
        lax.all_gather(query_weight, "shard", axis=0, tiled=True),
        lax.all_gather(query_bias, "shard", axis=0, tiled=True),
        lax.all_gather(key_weight, "shard", axis=0, tiled=True),
        lax.all_gather(key_bias, "shard", axis=0, tiled=True),
        lax.all_gather(value_weight, "shard", axis=0, tiled=True),
        lax.all_gather(value_bias, "shard", axis=0, tiled=True),
        lax.all_gather(out_weight, "shard", axis=0, tiled=True),
        lax.all_gather(second_gain, "shard", axis=0, tiled=True),
        lax.all_gather(gate_weight, "shard", axis=0, tiled=True),
        lax.all_gather(up_weight, "shard", axis=0, tiled=True),
        lax.all_gather(down_weight, "shard", axis=0, tiled=True),
    )
    (
        gain_first,
        query_matrix,
        query_vector,
        key_matrix,
        key_vector,
        value_matrix,
        value_vector,
        output_matrix,
        gain_second,
        gate_matrix,
        up_matrix,
        down_matrix,
    ) = gathered
    query_width = query_matrix.shape[1]
    key_width = key_matrix.shape[1]
    head_count = query_width // HD
    shared_heads = key_width // HD
    group_size = head_count // shared_heads
    block_seqs = math.gcd(sequences, max(1, 512 // local_tokens))
    block_count = sequences // block_seqs

    def split(values):
        return values.reshape((block_count, block_seqs) + values.shape[1:])

    all_segments = lax.all_gather(segments, "shard", axis=1, tiled=True)
    full_length = all_segments.shape[1]
    offset = lax.axis_index("shard") * local_tokens
    places = offset + jnp.arange(local_tokens, dtype=jnp.int32)
    earlier = jnp.sum((all_segments[:, None, :] < segments[:, :, None]).astype(jnp.int32), axis=2)
    position = places[None, :] - earlier
    frequency = jnp.power(THETA, -(jnp.arange(HD // 2, dtype=jnp.float32) * 2.0 / HD))
    angles = position.reshape(row_count).astype(jnp.float32)[:, None] * frequency[None, :]
    cosine = jnp.cos(angles)
    sine_table = jnp.sin(angles)
    causal = places[:, None] >= jnp.arange(full_length, dtype=jnp.int32)[None, :]
    allowed = (segments[:, :, None] == all_segments[:, None, :]) & causal[None]
    inputs = tokens.astype(jnp.float32).reshape(row_count, model_width)
    scale_first = rms_scale(inputs)
    normed_first = (inputs * scale_first * gain_first.astype(jnp.float32)).astype(jnp.bfloat16)
    query_linear = jnp.dot(
        normed_first, query_matrix, preferred_element_type=jnp.float32
    ) + query_vector.astype(jnp.float32)
    key_linear = jnp.dot(
        normed_first, key_matrix, preferred_element_type=jnp.float32
    ) + key_vector.astype(jnp.float32)
    values_local = (
        jnp.dot(normed_first, value_matrix, preferred_element_type=jnp.float32)
        + value_vector.astype(jnp.float32)
    ).astype(jnp.bfloat16)
    queries = rotate(query_linear.reshape(row_count, head_count, HD), cosine, sine_table).astype(
        jnp.bfloat16
    )
    keys_local = rotate(key_linear.reshape(row_count, shared_heads, HD), cosine, sine_table).astype(
        jnp.bfloat16
    )
    keys_all, values_all = (
        lax.all_gather(
            keys_local.reshape(sequences, local_tokens, key_width), "shard", axis=1, tiled=True
        ),
        lax.all_gather(
            values_local.reshape(sequences, local_tokens, key_width), "shard", axis=1, tiled=True
        ),
    )
    queries_grouped = queries.reshape(sequences, local_tokens, shared_heads, group_size, HD)
    keys_heads = keys_all.reshape(sequences, full_length, shared_heads, HD)
    values_heads = values_all.reshape(sequences, full_length, shared_heads, HD)
    mixed_blocks, log_blocks = lax.map(
        attend, (split(queries_grouped), split(keys_heads), split(values_heads), split(allowed))
    )
    mixed_heads = mixed_blocks.reshape(row_count, query_width)
    hidden = inputs + jnp.dot(mixed_heads, output_matrix, preferred_element_type=jnp.float32)
    scale_second = rms_scale(hidden)
    normed_second = (hidden * scale_second * gain_second.astype(jnp.float32)).astype(jnp.bfloat16)
    gate_linear = jnp.dot(normed_second, gate_matrix, preferred_element_type=jnp.float32)
    up_linear = jnp.dot(normed_second, up_matrix, preferred_element_type=jnp.float32)
    sigmoid_gate = jax.nn.sigmoid(gate_linear)
    activation = (gate_linear * sigmoid_gate * up_linear).astype(jnp.bfloat16)
    output = (
        (hidden + jnp.dot(activation, down_matrix, preferred_element_type=jnp.float32))
        .astype(jnp.bfloat16)
        .reshape(tokens.shape)
    )
    backward_set = (
        lax.all_gather(first_gain, "shard", axis=0, tiled=True),
        lax.all_gather(query_weight, "shard", axis=0, tiled=True),
        lax.all_gather(key_weight, "shard", axis=0, tiled=True),
        lax.all_gather(value_weight, "shard", axis=0, tiled=True),
        lax.all_gather(out_weight, "shard", axis=0, tiled=True),
        lax.all_gather(second_gain, "shard", axis=0, tiled=True),
        lax.all_gather(gate_weight, "shard", axis=0, tiled=True),
        lax.all_gather(up_weight, "shard", axis=0, tiled=True),
        lax.all_gather(down_weight, "shard", axis=0, tiled=True),
    )
    (
        gain_first,
        query_matrix,
        key_matrix,
        value_matrix,
        output_matrix,
        gain_second,
        gate_matrix,
        up_matrix,
        down_matrix,
    ) = backward_set
    grad_output = cotangent.reshape(row_count, model_width)
    grad_activation = times_transposed(grad_output, down_matrix)
    gate_slope = sigmoid_gate + gate_linear * sigmoid_gate * (1.0 - sigmoid_gate)
    grad_gate = (grad_activation * up_linear * gate_slope).astype(jnp.bfloat16)
    grad_up = (grad_activation * gate_linear * sigmoid_gate).astype(jnp.bfloat16)
    grad_normed = times_transposed(grad_gate, gate_matrix) + times_transposed(grad_up, up_matrix)
    second_gain_grad = jnp.sum(grad_normed * hidden * scale_second, axis=0)
    grad_hidden = grad_output.astype(jnp.float32) + norm_back(
        grad_normed, hidden, scale_second, gain_second
    )
    grad_branch = grad_hidden.astype(jnp.bfloat16)
    out_grad = inner_rows(mixed_heads, grad_branch)
    grad_mixed = times_transposed(grad_branch, output_matrix).astype(jnp.bfloat16)
    grad_mixed = grad_mixed.reshape(sequences, local_tokens, shared_heads, group_size, HD)
    grad_query_blocks, grad_key_blocks, grad_value_blocks = lax.map(
        attend_back,
        (
            split(queries_grouped),
            split(keys_heads),
            split(values_heads),
            split(allowed),
            log_blocks,
            split(grad_mixed),
        ),
    )
    grad_queries_rot = grad_query_blocks.reshape(row_count, head_count, HD)
    grad_keys_part = grad_key_blocks.reshape(sequences, full_length, key_width)
    grad_values_part = grad_value_blocks.reshape(sequences, full_length, key_width)
    grad_keys_sum, grad_values_sum = (
        lax.psum_scatter(
            grad_keys_part.astype(jnp.bfloat16), "shard", scatter_dimension=1, tiled=True
        ).astype(jnp.float32),
        lax.psum_scatter(
            grad_values_part.astype(jnp.bfloat16), "shard", scatter_dimension=1, tiled=True
        ).astype(jnp.float32),
    )
    grad_queries = (
        rotate(grad_queries_rot, cosine, -sine_table)
        .astype(jnp.bfloat16)
        .reshape(row_count, query_width)
    )
    grad_keys = (
        rotate(grad_keys_sum.reshape(row_count, shared_heads, HD), cosine, -sine_table)
        .astype(jnp.bfloat16)
        .reshape(row_count, key_width)
    )
    grad_values = grad_values_sum.reshape(row_count, key_width).astype(jnp.bfloat16)
    query_grad = inner_rows(normed_first, grad_queries)
    key_grad = inner_rows(normed_first, grad_keys)
    value_grad = inner_rows(normed_first, grad_values)
    query_bias_grad = jnp.sum(grad_queries.astype(jnp.float32), axis=0)
    key_bias_grad = jnp.sum(grad_keys.astype(jnp.float32), axis=0)
    value_bias_grad = jnp.sum(grad_values.astype(jnp.float32), axis=0)
    grad_first = (
        times_transposed(grad_queries, query_matrix)
        + times_transposed(grad_keys, key_matrix)
        + times_transposed(grad_values, value_matrix)
    )
    first_gain_grad = jnp.sum(grad_first * inputs * scale_first, axis=0)
    tokens_grad = (
        (grad_hidden + norm_back(grad_first, inputs, scale_first, gain_first))
        .astype(jnp.bfloat16)
        .reshape(tokens.shape)
    )
    down_grad = inner_rows(activation, grad_output)
    gate_grad = inner_rows(normed_second, grad_gate)
    up_grad = inner_rows(normed_second, grad_up)
    owned_grads = (
        lax.psum_scatter(
            first_gain_grad.astype(jnp.bfloat16), "shard", scatter_dimension=0, tiled=True
        ).astype(jnp.float32),
        lax.psum_scatter(
            query_grad.astype(jnp.bfloat16), "shard", scatter_dimension=0, tiled=True
        ).astype(jnp.float32),
        lax.psum_scatter(
            query_bias_grad.astype(jnp.bfloat16), "shard", scatter_dimension=0, tiled=True
        ).astype(jnp.float32),
        lax.psum_scatter(
            key_grad.astype(jnp.bfloat16), "shard", scatter_dimension=0, tiled=True
        ).astype(jnp.float32),
        lax.psum_scatter(
            key_bias_grad.astype(jnp.bfloat16), "shard", scatter_dimension=0, tiled=True
        ).astype(jnp.float32),
        lax.psum_scatter(
            value_grad.astype(jnp.bfloat16), "shard", scatter_dimension=0, tiled=True
        ).astype(jnp.float32),
        lax.psum_scatter(
            value_bias_grad.astype(jnp.bfloat16), "shard", scatter_dimension=0, tiled=True
        ).astype(jnp.float32),
        lax.psum_scatter(
            out_grad.astype(jnp.bfloat16), "shard", scatter_dimension=0, tiled=True
        ).astype(jnp.float32),
        lax.psum_scatter(
            second_gain_grad.astype(jnp.bfloat16), "shard", scatter_dimension=0, tiled=True
        ).astype(jnp.float32),
        lax.psum_scatter(
            gate_grad.astype(jnp.bfloat16), "shard", scatter_dimension=0, tiled=True
        ).astype(jnp.float32),
        lax.psum_scatter(
            up_grad.astype(jnp.bfloat16), "shard", scatter_dimension=0, tiled=True
        ).astype(jnp.float32),
        lax.psum_scatter(
            down_grad.astype(jnp.bfloat16), "shard", scatter_dimension=0, tiled=True
        ).astype(jnp.float32),
    )
    summed = (
        lax.psum(owned_grads[0].astype(jnp.bfloat16), "rep").astype(jnp.float32),
        lax.psum(owned_grads[1].astype(jnp.bfloat16), "rep").astype(jnp.float32),
        lax.psum(owned_grads[2].astype(jnp.bfloat16), "rep").astype(jnp.float32),
        lax.psum(owned_grads[3].astype(jnp.bfloat16), "rep").astype(jnp.float32),
        lax.psum(owned_grads[4].astype(jnp.bfloat16), "rep").astype(jnp.float32),
        lax.psum(owned_grads[5].astype(jnp.bfloat16), "rep").astype(jnp.float32),
        lax.psum(owned_grads[6].astype(jnp.bfloat16), "rep").astype(jnp.float32),
        lax.psum(owned_grads[7].astype(jnp.bfloat16), "rep").astype(jnp.float32),
        lax.psum(owned_grads[8].astype(jnp.bfloat16), "rep").astype(jnp.float32),
        lax.psum(owned_grads[9].astype(jnp.bfloat16), "rep").astype(jnp.float32),
        lax.psum(owned_grads[10].astype(jnp.bfloat16), "rep").astype(jnp.float32),
        lax.psum(owned_grads[11].astype(jnp.bfloat16), "rep").astype(jnp.float32),
    )
    return (
        output,
        tokens_grad,
        summed[0],
        summed[1],
        summed[2],
        summed[3],
        summed[4],
        summed[5],
        summed[6],
        summed[7],
        summed[8],
        summed[9],
        summed[10],
        summed[11],
    )


def solution(mesh):
    placed = (
        P("rep", "shard", None),
        P("rep", "shard"),
        P("shard"),
        P("shard", None),
        P("shard"),
        P("shard", None),
        P("shard"),
        P("shard", None),
        P("shard"),
        P("shard", None),
        P("shard"),
        P("shard", None),
        P("shard", None),
        P("shard", None),
        P("rep", "shard", None),
    )
    return jax.shard_map(
        on_device,
        mesh=mesh,
        in_specs=placed,
        out_specs=(
            P("rep", "shard", None),
            P("rep", "shard", None),
            P("shard"),
            P("shard", None),
            P("shard"),
            P("shard", None),
            P("shard"),
            P("shard", None),
            P("shard"),
            P("shard", None),
            P("shard"),
            P("shard", None),
            P("shard", None),
            P("shard", None),
        ),
        check_vma=False,
    )
```

profile of v0, /device:TPU:0, one launch (start us, length us, event | category | flops | bytes accessed | tf_op | source)
XLA Modules:
  0.0 1725.7 jit_solution(14594317526729918583)
XLA Ops:
  15.5 23.4 %all-reduce.11 = (bf16[896]{0:T(1024)(128)(2,1)S(1)}, bf16[128]{0:T(256)(128)(2,1)S(1)}, bf16[128]{0:T(256)(128)(2,1)S(1)}, bf16[896]{0:T(1024)(128)(2,1)S(1)}, bf16[896]{0:T(1024)(128)(2,1)S(1)}) all-reduce(bf16[896]{0:T(1024)(128)(2,1)S(1)} %dynamic-update-slice, ...), channel_id=1, replica_groups=mesh['rep'=4,'shard'=8] {'shard'}, use_global_device_ids=true, to_apply=%add | all-reduce | flops 2944 | bytes 11776
  39.5 30.9 %all_gather.55 = bf16[896,128]{1,0:T(8,128)(2,1)S(1)} all-gather(bf16[112,128]{1,0:T(8,128)(2,1)} %param.22), channel_id=1, replica_groups=mesh['rep'=4,'shard'=8] {'shard'}, dimensions={0}, use_global_device_ids=true | all-gather | bytes 258048 | tf_op jit(solution)/shard_map/all_gather | solution.py:122
  73.9 26.2 %all_gather.58 = s32[2,2048]{1,0:T(2,128)S(1)} all-gather(s32[2,256]{1,0:T(2,128)} %param.16), channel_id=1, replica_groups=mesh['rep'=4,'shard'=8] {'shard'}, dimensions={1}, use_global_device_ids=true | all-gather | bytes 18432 | tf_op jit(solution)/shard_map/all_gather | solution.py:155
  101.7 31.3 %all_gather.59 = bf16[896,128]{1,0:T(8,128)(2,1)S(1)} all-gather(bf16[112,128]{1,0:T(8,128)(2,1)} %param.20), channel_id=1, replica_groups=mesh['rep'=4,'shard'=8] {'shard'}, dimensions={0}, use_global_device_ids=true | all-gather | bytes 258048 | tf_op jit(solution)/shard_map/all_gather | solution.py:120
  142.1 14.4 all-gather.12.cloned.1.call-done
  164.7 32.8 %all-gather.10.cloned.1.call-done = bf16[2,2048,128]{1,2,0:T(8,128)(2,1)} async-done(((bf16[2,256,128]{1,2,0:T(8,128)(2,1)}), bf16[2,2048,128]{1,2,0:T(8,128)(2,1)}) %all-gather.10.cloned.1.call-update) | async-done | bytes 1048592 | tf_op jit(solution)/shard_map/all_gather | solution.py:187
  197.5 21.8 %fusion.9 = (f32[2,2,7,256]{3,2,1,0:T(8,128)S(1)}, f32[2,2,2048,256,7]{3,2,4,1,0:T(8,128)}) fusion(pred[2,256,2048]{1,2,0:T(8,128)(4,1)S(1)} %compare_and_fusion, bf16[2,2048,2,64,1]{1,3,4,2,0:T(8,128)(2,1)} %bitcast.183, bf16[2,256,2,7,64]{1,4,3,2,0:T(8,128)(2,1)S(1)} %copy_dynamic-update-slice_fusion), kind=kOutput, calls=%fused_computation.14 | convolution fusion | flops 1923081216 | bytes 61763584 | tf_op jit(solution)/shard_map/while/body/eval_jaxpr/bqkgd,bskd->bkgqs/dot_general | solution.py:56
  219.4 19.4 %fusion.3 = f32[2,2,7,256]{3,2,1,0:T(8,128)S(1)} fusion(f32[2,2,7,256]{3,2,1,0:T(8,128)S(1)} %get-tuple-element.113, f32[2,2,2048,256,7]{3,2,4,1,0:T(8,128)} %get-tuple-element.114, pred[2,256,2048]{1,2,0:T(8,128)(4,1)S(1)} %compare_and_fusion), kind=kLoop, calls=%fused_computation.9 | loop fusion | flops 58713088 | bytes 59826176 | tf_op jit(solution)/shard_map/while/body/eval_jaxpr/reduce_sum | solution.py:67
  238.8 24.0 %fusion.34 = bf16[2,256,2,7,64]{1,4,3,2,0:T(8,128)(2,1)S(1)} fusion(bf16[2,2048,2,64,1]{1,3,4,2,0:T(8,128)(2,1)S(1)} %bitcast.186, f32[2,2,7,256]{3,2,1,0:T(8,128)S(1)} %fusion.3, f32[2,2,7,256]{3,2,1,0:T(8,128)S(1)} %get-tuple-element.113, f32[2,2,2048,256,7]{3,2,4,1,0:T(8,128)} %get-tuple-element.114, pred[2,256,2048]{1,2,0:T(8,128)(4,1)S(1)} %compare_and_fusion), kind=kOutput, calls=%fused_computation.65 | convolution fusion | flops 1952907264 | bytes 61792256 | tf_op jit(solution)/shard_map/while/body/eval_jaxpr/bkgqs,bskd->bqkgd/dot_general | solution.py:69
  268.6 104.3 %all-gather.18.cloned.1.call-done = bf16[896,4864]{1,0:T(8,128)(2,1)} async-done(((bf16[112,4864]{1,0:T(8,128)(2,1)}), bf16[896,4864]{1,0:T(8,128)(2,1)}) %all-gather.18.cloned.1.call-update) | async-done | bytes 8716304 | tf_op jit(solution)/shard_map/all_gather | solution.py:127
  384.1 118.4 %all-gather.16.cloned.1.call-done = bf16[896,4864]{1,0:T(8,128)(2,1)} async-done(((bf16[112,4864]{1,0:T(8,128)(2,1)}), bf16[896,4864]{1,0:T(8,128)(2,1)}) %all-gather.16.cloned.1.call-update) | async-done | bytes 8716304 | tf_op jit(solution)/shard_map/all_gather | solution.py:126
  502.4 11.4 fusion.48
  513.8 118.3 %all-gather.20.cloned.1.call-done = bf16[4864,896]{1,0:T(8,128)(2,1)} async-done(((bf16[608,896]{1,0:T(8,128)(2,1)}), bf16[4864,896]{1,0:T(8,128)(2,1)}) %all-gather.20.cloned.1.call-update) | async-done | bytes 8716304 | tf_op jit(solution)/shard_map/all_gather | solution.py:128
  632.1 19.0 %multiply_convert_fusion = (bf16[512,4864]{1,0:T(8,128)(2,1)}, bf16[512,4864]{1,0:T(8,128)(2,1)}, bf16[512,4864]{1,0:T(8,128)(2,1)}) fusion(f32[512,4864]{1,0:T(8,128)} %fusion.48, f32[512,4864]{1,0:T(8,128)} %fusion.49, bf16[512,896]{1,0:T(8,128)(2,1)S(1)} %bitcast.194, bf16[4864,896]{1,0:T(8,128)(2,1)} %all-gather.20.cloned.1.call-done), kind=kOutput, calls=%fused_computation.15 | convolution fusion | flops 4500094976 | bytes 44498944 | tf_op jit(solution)/shard_map/dot_general | solution.py:42
  651.2 12.2 fusion.50
  663.5 11.6 multiply_reduce_fusion
  684.3 39.0 %fusion = (f32[2,2,7,256]{3,2,1,0:T(8,128)S(1)}, f32[2,2,2048,256,7]{3,2,4,1,0:T(8,128)}) fusion(f32[2,2,7,256]{3,2,1,0:T(8,128)S(1)} %log_add_fusion, f32[2,2,2048,256,7]{3,2,4,1,0:T(8,128)} %get-tuple-element.114, pred[2,256,2048]{1,2,0:T(8,128)(4,1)S(1)} %compare_and_fusion, bf16[2,2048,2,64,1]{1,3,4,2,0:T(8,128)(2,1)} %bitcast.185, ...), kind=kOutput, calls=%fused_computation.2 | convolution fusion | flops 1952441344 | bytes 120512512 | tf_op jit(solution)/shard_map/while/body/eval_jaxpr/bqkgd,bskd->bkgqs/dot_general | solution.py:77
  723.3 46.7 %fusion.2 = bf16[2,2,7,256,2048]{3,4,2,1,0:T(8,128)(2,1)} fusion(f32[2,2,2048,256,7]{3,2,4,1,0:T(8,128)} %get-tuple-element.119, f32[2,2,7,256]{3,2,1,0:T(8,128)S(1)} %get-tuple-element.118, f32[2,2,7,256]{3,2,1,0:T(8,128)S(1)} %log_add_fusion, f32[2,2,2048,256,7]{3,2,4,1,0:T(8,128)} %get-tuple-element.114, pred[2,256,2048]{1,2,0:T(8,128)(4,1)S(1)} %compare_and_fusion), kind=kLoop, calls=%fused_computation.4 | loop fusion | flops 88080384 | bytes 147906560 | tf_op jit(solution)/shard_map/while/body/eval_jaxpr/convert_element_type | solution.py:81
  770.0 15.4 fusion.15
  785.5 23.2 %fusion.16 = bf16[2,2,64,2048]{3,2,1,0:T(8,128)(2,1)} fusion(bf16[2,256,2,7,64]{1,4,3,2,0:T(8,128)(2,1)} %copy.68, f32[2,2,7,256]{3,2,1,0:T(8,128)S(1)} %log_add_fusion, f32[2,2,2048,256,7]{3,2,4,1,0:T(8,128)} %get-tuple-element.114, pred[2,256,2048]{1,2,0:T(8,128)(4,1)S(1)} %compare_and_fusion), kind=kOutput, calls=%fused_computation.29 | convolution fusion | flops 1938292736 | bytes 61763584 | tf_op jit(solution)/shard_map/while/body/eval_jaxpr/bkgqs,bqkgd->bskd/dot_general | solution.py:88
  815.2 12.3 multiply_bitcast_fusion
  873.2 40.7 %reduce-scatter.12.cloned.1.call-done = bf16[2,256,128]{2,1,0:T(8,128)(2,1)} async-done(((bf16[2,2048,128]{2,1,0:T(8,128)(2,1)}), bf16[2,256,128]{2,1,0:T(8,128)(2,1)}) %reduce-scatter.12.cloned.1.call-update) | async-done | bytes 131088 | tf_op jit(solution)/shard_map/reduce_scatter | solution.py:267
  918.9 61.0 %reduce-scatter.20.cloned.1.call-done = bf16[112,896]{1,0:T(8,128)(2,1)} async-done(((bf16[896,896]{1,0:T(8,128)(2,1)}), bf16[112,896]{1,0:T(8,128)(2,1)}) %reduce-scatter.20.cloned.1.call-update) | async-done | bytes 200720 | tf_op jit(solution)/shard_map/reduce_scatter | solution.py:324
  979.9 67.1 %reduce-scatter.14.cloned.1.call-done = bf16[112,896]{1,0:T(8,128)(2,1)} async-done(((bf16[896,896]{1,0:T(8,128)(2,1)}), bf16[112,896]{1,0:T(8,128)(2,1)}) %reduce-scatter.14.cloned.1.call-update) | async-done | bytes 200720 | tf_op jit(solution)/shard_map/reduce_scatter | solution.py:306
  1047.0 156.4 %reduce-scatter.24.cloned.1.call-done = bf16[112,4864]{1,0:T(8,128)(2,1)} async-done(((bf16[896,4864]{1,0:T(8,128)(2,1)}), bf16[112,4864]{1,0:T(8,128)(2,1)}) %reduce-scatter.24.cloned.1.call-update) | async-done | bytes 1089552 | tf_op jit(solution)/shard_map/reduce_scatter | solution.py:333
  1203.4 156.7 %reduce-scatter.22.cloned.1.call-done = bf16[112,4864]{1,0:T(8,128)(2,1)} async-done(((bf16[896,4864]{1,0:T(8,128)(2,1)}), bf16[112,4864]{1,0:T(8,128)(2,1)}) %reduce-scatter.22.cloned.1.call-update) | async-done | bytes 1089552 | tf_op jit(solution)/shard_map/reduce_scatter | solution.py:330
  1360.1 156.6 %reduce-scatter.26.cloned.1.call-done = bf16[608,896]{1,0:T(8,128)(2,1)} async-done(((bf16[4864,896]{1,0:T(8,128)(2,1)}), bf16[608,896]{1,0:T(8,128)(2,1)}) %reduce-scatter.26.cloned.1.call-update) | async-done | bytes 1089552 | tf_op jit(solution)/shard_map/reduce_scatter | solution.py:336
  1535.9 19.8 %all-reduce.10 = (bf16[896]{0:T(1024)(128)(2,1)S(1)}, bf16[896]{0:T(1024)(128)(2,1)S(1)}, bf16[128]{0:T(256)(128)(2,1)S(1)}, bf16[128]{0:T(256)(128)(2,1)S(1)}, bf16[896]{0:T(1024)(128)(2,1)S(1)}) all-reduce(bf16[896]{0:T(1024)(128)(2,1)S(1)} %get-tuple-element.57, ...), channel_id=4, replica_groups=mesh['rep'=4,'shard'=8] {'shard'}, use_global_device_ids=true, to_apply=%region_11.12.clone | all-reduce | flops 2944 | bytes 11776
  1558.9 14.3 reduce-scatter.18.cloned.1.call-done
  1573.3 56.9 %reduce-scatter.16.cloned.1.call-done = bf16[112,128]{1,0:T(8,128)(2,1)} async-done(((bf16[896,128]{1,0:T(8,128)(2,1)}), bf16[112,128]{1,0:T(8,128)(2,1)}) %reduce-scatter.16.cloned.1.call-update) | async-done | bytes 28688 | tf_op jit(solution)/shard_map/reduce_scatter | solution.py:312
  1630.1 11.8 all-reduce.12
  1645.8 63.9 %all-reduce.16.cloned.1.call-done = (bf16[112,896]{1,0:T(8,128)(2,1)}, bf16[112,896]{1,0:T(8,128)(2,1)}, bf16[112,4864]{1,0:T(8,128)(2,1)}, bf16[112,4864]{1,0:T(8,128)(2,1)}, bf16[608,896]{1,0:T(8,128)(2,1)}) async-done(((bf16[112,896]{1,0:T(8,128)(2,1)}, bf16[112,896]{1,0:T(8,128)(2,1)}, bf16[112,4864]{1,0:T(8,128)(2,1)}, bf16[112,4864]{1,0:T(8,128)(2,1)}, bf16[608,896]{1,0:T(8,128)(2,1)}), ...) | async-done | bytes 3670032 | tf_op jit(solution)/shard_map/psum | solution.py:342
  (206 shorter events, 147.1 us)
Async XLA Ops:
  7.2 132.7 %all-gather.8.cloned.1.call-start = ((), (), s32[]{:S(2)}) async-start(), calls=%async_computation.9 | async-start | bytes 1179648 | tf_op jit(solution)/shard_map/all_gather | solution.py:190
  38.9 34.1 %copy-start.27 = (f32[896]{0:T(1024)}, f32[896]{0:T(1024)S(1)}, u32[]{:S(2)}) copy-start(f32[896]{0:T(1024)S(1)} %convert_element_type.249) | copy-start | bytes 10756
  39.5 33.5 %copy-start.29 = (f32[1,2,2,128]{3,1,2,0:T(2,128)}, f32[1,2,2,128]{3,1,2,0:T(2,128)S(1)}, u32[]{:S(2)}) copy-start(f32[1,2,2,128]{3,1,2,0:T(2,128)S(1)} %copy.88) | copy-start | bytes 6148
  70.4 68.3 %copy-start.31 = (s32[2,256]{1,0:T(2,128)S(1)}, s32[2,256]{1,0:T(2,128)}, u32[]{:S(2)}) copy-start(s32[2,256]{1,0:T(2,128)} %param.16) | copy-start | bytes 6148
  73.1 83.5 %all-gather.12.cloned.1.call-start = ((), (), s32[]{:S(2)}) async-start(), calls=%async_computation.11 | async-start | bytes 1806336 | tf_op jit(solution)/shard_map/all_gather | solution.py:118
  73.8 123.7 %all-gather.10.cloned.1.call-start = ((), (), s32[]{:S(2)}) async-start(), calls=%async_computation.10 | async-start | bytes 1179648 | tf_op jit(solution)/shard_map/all_gather | solution.py:187
  134.0 28.2 %copy-start.14 = (f32[512,32]{0,1:T(8,128)}, f32[512,32]{0,1:T(8,128)S(1)}, u32[]{:S(2)}) copy-start(f32[512,32]{0,1:T(8,128)S(1)} %get-tuple-element.108) | copy-start | bytes 196612
  135.2 128.8 %all-gather.14.cloned.1.call-start = ((), (), s32[]{:S(2)}) async-start(), calls=%async_computation.12 | async-start | bytes 1806336 | tf_op jit(solution)/shard_map/all_gather | solution.py:124
  135.8 237.1 %all-gather.18.cloned.1.call-start = ((), (), s32[]{:S(2)}) async-start(), calls=%async_computation.14 | async-start | bytes 9805824 | tf_op jit(solution)/shard_map/all_gather | solution.py:127
  136.4 366.0 %all-gather.16.cloned.1.call-start = ((), (), s32[]{:S(2)}) async-start(), calls=%async_computation.13 | async-start | bytes 9805824 | tf_op jit(solution)/shard_map/all_gather | solution.py:126
  137.0 495.2 %all-gather.20.cloned.1.call-start = ((), (), s32[]{:S(2)}) async-start(), calls=%async_computation.15 | async-start | bytes 9805824 | tf_op jit(solution)/shard_map/all_gather | solution.py:128
  137.7 734.2 %reduce-scatter.10.cloned.1.call-start = ((), (), s32[]{:S(2)}) async-start(), calls=%async_computation.16 | async-start | bytes 1179648 | tf_op jit(solution)/shard_map/reduce_scatter | solution.py:264
  164.7 54.7 %copy-start.7 = (bf16[2,256,2,7,64]{1,4,3,2,0:T(8,128)(2,1)}, bf16[2,256,2,7,64]{1,4,3,2,0:T(8,128)(2,1)S(1)}, u32[]{:S(2)}) copy-start(bf16[2,256,2,7,64]{1,4,3,2,0:T(8,128)(2,1)S(1)} %copy_dynamic-update-slice_fusion) | copy-start | bytes 2752516
  219.4 19.4 %copy-start.9 = (bf16[2,2048,128]{1,2,0:T(8,128)(2,1)S(1)}, bf16[2,2048,128]{1,2,0:T(8,128)(2,1)}, u32[]{:S(2)}) copy-start(bf16[2,2048,128]{1,2,0:T(8,128)(2,1)} %copy.60) | copy-start | bytes 3145732
  238.8 25.3 %copy-start = (bf16[2,256,896]{2,1,0:T(8,128)(2,1)S(1)}, bf16[2,256,896]{2,1,0:T(8,128)(2,1)}, u32[]{:S(2)}) copy-start(bf16[2,256,896]{2,1,0:T(8,128)(2,1)} %param.15) | copy-start | bytes 2752516
  264.0 120.1 %copy-start.23 = (bf16[112,8,2,256]{3,1,2,0:T(8,128)(2,1)}, bf16[112,8,2,256]{3,1,2,0:T(8,128)(2,1)S(1)}, u32[]{:S(2)}) copy-start(bf16[112,8,2,256]{3,1,2,0:T(8,128)(2,1)S(1)} %copy.90) | copy-start | bytes 2752516
  268.6 104.3 %copy-start.24 = (bf16[512,896]{1,0:T(8,128)(2,1)}, bf16[512,896]{1,0:T(8,128)(2,1)S(1)}, u32[]{:S(2)}) copy-start(bf16[512,896]{1,0:T(8,128)(2,1)S(1)} %multiply_convert_fusion.3) | copy-start | bytes 2752516
  384.1 248.1 %copy-start.19 = (bf16[2,256,896]{2,1,0:T(8,128)(2,1)S(1)}, bf16[2,256,896]{2,1,0:T(8,128)(2,1)}, u32[]{:S(2)}) copy-start(bf16[2,256,896]{2,1,0:T(8,128)(2,1)} %param.29) | copy-start | bytes 2752516
  651.2 12.2 copy-start.3
  651.2 12.3 copy-start.35
  723.3 46.7 %copy-start.8 = (bf16[2,256,2,7,64]{1,4,3,2,0:T(8,128)(2,1)S(1)}, bf16[2,256,2,7,64]{1,4,3,2,0:T(8,128)(2,1)}, u32[]{:S(2)}) copy-start(bf16[2,256,2,7,64]{1,4,3,2,0:T(8,128)(2,1)} %copy-done.7) | copy-start | bytes 2752516
  785.4 25.7 %copy-start.5 = (f32[512,896]{1,0:T(8,128)S(1)}, f32[512,896]{1,0:T(8,128)}, u32[]{:S(2)}) copy-start(f32[512,896]{1,0:T(8,128)} %copy-done.4) | copy-start | bytes 5505028
  785.5 128.4 %reduce-scatter.12.cloned.1.call-start = ((), (), s32[]{:S(2)}) async-start(), calls=%async_computation.17 | async-start | bytes 1179648 | tf_op jit(solution)/shard_map/reduce_scatter | solution.py:267
  811.1 168.8 %reduce-scatter.20.cloned.1.call-start = ((), (), s32[]{:S(2)}) async-start(), calls=%async_computation.21 | async-start | bytes 1806336 | tf_op jit(solution)/shard_map/reduce_scatter | solution.py:324
  814.6 232.4 %reduce-scatter.14.cloned.1.call-start = ((), (), s32[]{:S(2)}) async-start(), calls=%async_computation.18 | async-start | bytes 1806336 | tf_op jit(solution)/shard_map/reduce_scatter | solution.py:306
  839.2 364.2 %reduce-scatter.24.cloned.1.call-start = ((), (), s32[]{:S(2)}) async-start(), calls=%async_computation.23 | async-start | bytes 9805824 | tf_op jit(solution)/shard_map/reduce_scatter | solution.py:333
  849.8 510.3 %reduce-scatter.22.cloned.1.call-start = ((), (), s32[]{:S(2)}) async-start(), calls=%async_computation.22 | async-start | bytes 9805824 | tf_op jit(solution)/shard_map/reduce_scatter | solution.py:330
  860.7 656.0 %reduce-scatter.26.cloned.1.call-start = ((), (), s32[]{:S(2)}) async-start(), calls=%async_computation.24 | async-start | bytes 9805824 | tf_op jit(solution)/shard_map/reduce_scatter | solution.py:336
  871.8 701.4 %reduce-scatter.18.cloned.1.call-start = ((), (), s32[]{:S(2)}) async-start(), calls=%async_computation.20 | async-start | bytes 258048 | tf_op jit(solution)/shard_map/reduce_scatter | solution.py:318
  915.9 714.2 %reduce-scatter.16.cloned.1.call-start = ((), (), s32[]{:S(2)}) async-start(), calls=%async_computation.19 | async-start | bytes 258048 | tf_op jit(solution)/shard_map/reduce_scatter | solution.py:312
  917.3 792.4 %all-reduce.16.cloned.1.call-start = ((), (), s32[]{:S(2)}) async-start(), calls=%async_computation.25 | async-start | bytes 7340032 | tf_op jit(solution)/shard_map/psum | solution.py:342
  1531.7 24.4 %copy-start.6 = (f32[512,896]{1,0:T(8,128)S(1)}, f32[512,896]{1,0:T(8,128)}, u32[]{:S(2)}) copy-start(f32[512,896]{1,0:T(8,128)} %copy-done.4) | copy-start | bytes 5505028
  (21 other events, 92.4 us)
Sparse Core Ops, SparseCore 0:
  73.2 38.0 all-gather.7
  113.4 43.0 all-gather.11
  159.2 38.3 all-gather.9
  199.6 43.1 all-gather.13
  244.8 128.0 all-gather.17
  374.9 127.4 all-gather.15
  504.6 127.4 all-gather.19
  785.6 62.0 reduce-scatter.9
  851.4 62.3 reduce-scatter.11
  917.1 62.7 reduce-scatter.19
  984.4 62.6 reduce-scatter.13
  1050.5 152.8 reduce-scatter.23
  1207.0 153.0 reduce-scatter.21
  1363.6 153.0 reduce-scatter.25
  1519.7 53.5 reduce-scatter.17
  1576.6 53.4 reduce-scatter.15
  1632.7 76.9 all-reduce.15
where the time goes:
time: 1730 us
  waiting for transfers between devices  1160 us (67%)
  matrix products  271 us (16%)
  blocking collectives  143 us (8%)
  other arithmetic  94.2 us (5%)
  local copies, waits for them, and re-layouts  33.2 us (2%)
  between operations  17.4 us (1%)
    reduce_scatter x1, waiting for transfers between devices, on_device(): lax.psum_scatter(gate_grad.astype(jnp.bfloat16), 'shard', scatter_dimensi...  157 us
    reduce_scatter x1, waiting for transfers between devices, on_device(): lax.psum_scatter(down_grad.astype(jnp.bfloat16), 'shard', scatter_dimensi...  157 us
    reduce_scatter x1, waiting for transfers between devices, on_device(): lax.psum_scatter(up_grad.astype(jnp.bfloat16), 'shard', scatter_dimension...  156 us
    all_gather x1, waiting for transfers between devices, on_device(): lax.all_gather(gate_weight, 'shard', axis=0, tiled=True)  118 us
    all_gather x1, waiting for transfers between devices, on_device(): lax.all_gather(down_weight, 'shard', axis=0, tiled=True)  118 us
    all_gather x1, waiting for transfers between devices, on_device(): lax.all_gather(up_weight, 'shard', axis=0, tiled=True)  104 us
    reduce_scatter x1, waiting for transfers between devices, on_device(): lax.psum_scatter(query_grad.astype(jnp.bfloat16), 'shard', scatter_dimens...  67.1 us
    psum x1, waiting for transfers between devices, on_device(): lax.psum(owned_grads[1].astype(jnp.bfloat16), 'rep').astype(jnp.float32)  63.9 us
  transfers between devices with their start and end apart: 17, of which 14 were waited for; matrix products, arithmetic and copies ran while one was open for 13% of the time, Pallas kernels for 0%

commit v1 on v0

v1 whole, which is shorter than its diff:
```python
import functools
import math

import jax
import jax.numpy as jnp
from jax import lax
from jax.sharding import PartitionSpec as P

HD = 64


EPSILON = 1e-06
THETA = 1000000.0
MASKED = -1000000000.0


def rms_scale(values):
    return lax.rsqrt(jnp.mean(values * values, axis=-1, keepdims=True) + EPSILON)


def rotate(values, cosine, sine_table):
    half_size = values.shape[-1] // 2
    first_half = values[..., :half_size]
    second_half = values[..., half_size:]
    cosine = cosine[:, None, :]
    sine_table = sine_table[:, None, :]
    return jnp.concatenate(
        [
            first_half * cosine - second_half * sine_table,
            second_half * cosine + first_half * sine_table,
        ],
        axis=-1,
    )


def inner_rows(left_side, right_side):
    return lax.dot_general(
        left_side, right_side, (((0,), (0,)), ((), ())), preferred_element_type=jnp.float32
    )


def times_transposed(left_side, right_side):
    return lax.dot_general(
        left_side, right_side, (((1,), (1,)), ((), ())), preferred_element_type=jnp.float32
    )


def norm_back(grad_normed, values, scale_rows, gain_value):
    normal = values * scale_rows
    grad_scaled = grad_normed * gain_value.astype(jnp.float32)
    return scale_rows * (
        grad_scaled - normal * jnp.mean(grad_scaled * normal, axis=-1, keepdims=True)
    )


def masked_scores(query_block, key_block, mask_block):
    raw_scores = jnp.einsum(
        "bqkgd,bskd->bkgqs", query_block, key_block, preferred_element_type=jnp.float32
    ) * HD ** (-0.5)
    return jnp.where(mask_block[:, None, None], raw_scores, MASKED)


def attend(items):
    query_block, key_block, value_block, mask_block = items
    scores = masked_scores(query_block, key_block, mask_block)
    row_max = jnp.max(scores, axis=-1, keepdims=True)
    weights = jnp.exp(scores - row_max)
    row_total = jnp.sum(weights, axis=-1, keepdims=True)
    probs = (weights / row_total).astype(jnp.bfloat16)
    mixed = jnp.einsum("bkgqs,bskd->bqkgd", probs, value_block, preferred_element_type=jnp.float32)
    return (mixed.astype(jnp.bfloat16), row_max + jnp.log(row_total))


def attend_back(items):
    query_block, key_block, value_block, mask_block, log_block, grad_block = items
    scores = masked_scores(query_block, key_block, mask_block)
    probs_full = jnp.exp(scores - log_block)
    grad_probs = jnp.einsum(
        "bqkgd,bskd->bkgqs", grad_block, value_block, preferred_element_type=jnp.float32
    )
    row_delta = jnp.sum(probs_full * grad_probs, axis=-1, keepdims=True)
    grad_scores = (probs_full * (grad_probs - row_delta)).astype(jnp.bfloat16)
    grad_query = jnp.einsum(
        "bkgqs,bskd->bqkgd", grad_scores, key_block, preferred_element_type=jnp.float32
    ) * HD ** (-0.5)
    grad_key = jnp.einsum(
        "bkgqs,bqkgd->bskd", grad_scores, query_block, preferred_element_type=jnp.float32
    ) * HD ** (-0.5)
    grad_value = jnp.einsum(
        "bkgqs,bqkgd->bskd",
        probs_full.astype(jnp.bfloat16),
        grad_block,
        preferred_element_type=jnp.float32,
    )
    return (grad_query, grad_key, grad_value)


def pack_rows(pieces, width):
    flat = jnp.concatenate(pieces)
    rows = -(-flat.shape[0] // (8 * width)) * 8
    return jnp.pad(flat, (0, rows * width - flat.shape[0])).reshape(rows, width)


def on_device(
    tokens,
    segments,
    first_gain,
    query_weight,
    query_bias,
    key_weight,
    key_bias,
    value_weight,
    value_bias,
    out_weight,
    second_gain,
    gate_weight,
    up_weight,
    down_weight,
    cotangent,
    reps,
    shards,
):
    sequences, local_tokens, model_width = tokens.shape
    row_count = sequences * local_tokens
    own_rows = first_gain.shape[0]
    query_width = query_weight.shape[1]
    key_width = key_weight.shape[1]
    hidden_width = gate_weight.shape[1]
    own_hidden = down_weight.shape[0]
    part_hidden = own_hidden // reps
    slice_width = part_hidden * shards
    padded_width = -(-slice_width // 128) * 128
    qkv_width = query_width + 2 * key_width
    head_count = query_width // HD
    shared_heads = key_width // HD
    group_size = head_count // shared_heads
    block_seqs = math.gcd(sequences, max(1, 512 // local_tokens))
    block_count = sequences // block_seqs
    rep_index = lax.axis_index("rep")

    def split(values):
        return values.reshape((block_count, block_seqs) + values.shape[1:])

    def pick_columns(weight):
        grouped = weight.reshape(own_rows, shards, reps, part_hidden)
        picked = lax.dynamic_index_in_dim(grouped, rep_index, 2, keepdims=False)
        return picked.reshape(own_rows, slice_width)

    def widen(values):
        return jnp.pad(values, ((0, 0), (0, padded_width - slice_width)))

    small = pack_rows(
        [
            first_gain,
            second_gain,
            query_bias,
            key_bias,
            value_bias,
            segments.reshape(-1).astype(jnp.bfloat16),
        ],
        qkv_width,
    )
    qkv_part = jnp.concatenate([query_weight, key_weight, value_weight], axis=1)
    first_set = lax.all_gather(
        jnp.concatenate([qkv_part, small], axis=0), "shard", axis=0, tiled=False
    )
    qkv_matrix = first_set[:, :own_rows].reshape(model_width, qkv_width)
    small_set = first_set[:, own_rows:].reshape(shards, -1)
    sizes = [own_rows, own_rows, own_rows, key_bias.shape[0], value_bias.shape[0]]
    starts = [sum(sizes[:i]) for i in range(len(sizes) + 1)]
    gain_first, gain_second, query_vector, key_vector, value_vector = [
        small_set[:, starts[i] : starts[i] + sizes[i]].reshape(-1) for i in range(len(sizes))
    ]
    qkv_vector = jnp.concatenate([query_vector, key_vector, value_vector])
    all_segments = (
        small_set[:, starts[-1] : starts[-1] + row_count]
        .reshape(shards, sequences, local_tokens)
        .transpose(1, 0, 2)
        .reshape(sequences, shards * local_tokens)
        .astype(jnp.int32)
    )
    full_length = all_segments.shape[1]
    offset = lax.axis_index("shard") * local_tokens
    places = offset + jnp.arange(local_tokens, dtype=jnp.int32)
    earlier = jnp.sum((all_segments[:, None, :] < segments[:, :, None]).astype(jnp.int32), axis=2)
    position = places[None, :] - earlier
    frequency = jnp.power(THETA, -(jnp.arange(HD // 2, dtype=jnp.float32) * 2.0 / HD))
    angles = position.reshape(row_count).astype(jnp.float32)[:, None] * frequency[None, :]
    cosine = jnp.cos(angles)
    sine_table = jnp.sin(angles)
    causal = places[:, None] >= jnp.arange(full_length, dtype=jnp.int32)[None, :]
    allowed = (segments[:, :, None] == all_segments[:, None, :]) & causal[None]
    inputs = tokens.astype(jnp.float32).reshape(row_count, model_width)
    scale_first = rms_scale(inputs)
    normed_first = (inputs * scale_first * gain_first.astype(jnp.float32)).astype(jnp.bfloat16)
    linear = jnp.dot(
        normed_first, qkv_matrix, preferred_element_type=jnp.float32
    ) + qkv_vector.astype(jnp.float32)
    values_local = linear[:, query_width + key_width :].astype(jnp.bfloat16)
    rotated = rotate(
        linear[:, : query_width + key_width].reshape(row_count, head_count + shared_heads, HD),
        cosine,
        sine_table,
    ).astype(jnp.bfloat16)
    queries = rotated[:, :head_count]
    keys_local = rotated[:, head_count:].reshape(row_count, key_width)
    key_values = jnp.concatenate([keys_local, values_local], axis=1).reshape(
        sequences, local_tokens, 2 * key_width
    )
    later_part = jnp.concatenate(
        [out_weight, widen(pick_columns(gate_weight)), pick_columns(up_weight)], axis=1
    )
    down_part = lax.dynamic_slice_in_dim(down_weight, rep_index * part_hidden, part_hidden, 0)
    key_values, later_part, down_part, cotangent = lax.optimization_barrier(
        (key_values, later_part, down_part, cotangent)
    )
    key_values = lax.all_gather(key_values, "shard", axis=1, tiled=True)
    later_set = lax.all_gather(later_part, "shard", axis=0, tiled=True)
    down_matrix = lax.all_gather(down_part, "shard", axis=0, tiled=True)
    grad_output = cotangent.reshape(row_count, model_width)
    grad_output_all = lax.all_gather(grad_output, "rep", axis=0, tiled=True)
    output_matrix = later_set[:, :model_width]
    gate_matrix = later_set[:, model_width : model_width + slice_width]
    up_matrix = later_set[:, model_width + padded_width :]
    queries_grouped = queries.reshape(sequences, local_tokens, shared_heads, group_size, HD)
    keys_heads = key_values[:, :, :key_width].reshape(sequences, full_length, shared_heads, HD)
    values_heads = key_values[:, :, key_width:].reshape(sequences, full_length, shared_heads, HD)
    mixed_blocks, log_blocks = lax.map(
        attend, (split(queries_grouped), split(keys_heads), split(values_heads), split(allowed))
    )
    mixed_heads = mixed_blocks.reshape(row_count, query_width)
    hidden = inputs + jnp.dot(mixed_heads, output_matrix, preferred_element_type=jnp.float32)
    scale_second = rms_scale(hidden)
    normed_second = (hidden * scale_second * gain_second.astype(jnp.float32)).astype(jnp.bfloat16)
    normed_all = lax.all_gather(normed_second, "rep", axis=0, tiled=True)
    gate_linear = jnp.dot(normed_all, gate_matrix, preferred_element_type=jnp.float32)
    up_linear = jnp.dot(normed_all, up_matrix, preferred_element_type=jnp.float32)
    sigmoid_gate = jax.nn.sigmoid(gate_linear)
    activation = (gate_linear * sigmoid_gate * up_linear).astype(jnp.bfloat16)
    grad_activation = times_transposed(grad_output_all, down_matrix)
    gate_slope = sigmoid_gate + gate_linear * sigmoid_gate * (1.0 - sigmoid_gate)
    grad_gate = (grad_activation * up_linear * gate_slope).astype(jnp.bfloat16)
    grad_up = (grad_activation * gate_linear * sigmoid_gate).astype(jnp.bfloat16)
    grad_normed_part = (
        times_transposed(grad_gate, gate_matrix) + times_transposed(grad_up, up_matrix)
    ).astype(jnp.bfloat16)
    grad_normed = lax.psum_scatter(
        grad_normed_part, "rep", scatter_dimension=0, tiled=True
    ).astype(jnp.float32)
    down_grad = inner_rows(activation, grad_output_all).astype(jnp.bfloat16)
    gate_grad = inner_rows(normed_all, grad_gate).astype(jnp.bfloat16)
    up_grad = inner_rows(normed_all, grad_up).astype(jnp.bfloat16)
    down_owned = lax.psum_scatter(down_grad, "shard", scatter_dimension=0, tiled=True)
    second_gain_grad = jnp.sum(grad_normed * hidden * scale_second, axis=0)
    grad_hidden = grad_output.astype(jnp.float32) + norm_back(
        grad_normed, hidden, scale_second, gain_second
    )
    grad_branch = grad_hidden.astype(jnp.bfloat16)
    out_grad = inner_rows(mixed_heads, grad_branch).astype(jnp.bfloat16)
    later_owned = lax.psum_scatter(
        jnp.concatenate([out_grad, widen(gate_grad), up_grad], axis=1),
        "shard",
        scatter_dimension=0,
        tiled=True,
    )
    grad_mixed = times_transposed(grad_branch, output_matrix).astype(jnp.bfloat16)
    grad_mixed = grad_mixed.reshape(sequences, local_tokens, shared_heads, group_size, HD)
    grad_query_blocks, grad_key_blocks, grad_value_blocks = lax.map(
        attend_back,
        (
            split(queries_grouped),
            split(keys_heads),
            split(values_heads),
            split(allowed),
            log_blocks,
            split(grad_mixed),
        ),
    )
    output_part = jnp.dot(activation, down_matrix, preferred_element_type=jnp.float32)
    output = (
        (
            hidden
            + lax.psum_scatter(
                output_part.astype(jnp.bfloat16), "rep", scatter_dimension=0, tiled=True
            ).astype(jnp.float32)
        )
        .astype(jnp.bfloat16)
        .reshape(tokens.shape)
    )
    grad_queries_rot = grad_query_blocks.reshape(row_count, head_count, HD)
    grad_key_values = jnp.concatenate(
        [
            grad_key_blocks.astype(jnp.bfloat16).reshape(sequences, full_length, key_width),
            grad_value_blocks.astype(jnp.bfloat16).reshape(sequences, full_length, key_width),
        ],
        axis=2,
    )
    grad_key_values = lax.psum_scatter(
        grad_key_values, "shard", scatter_dimension=1, tiled=True
    ).reshape(row_count, 2 * key_width)
    grad_keys_sum = grad_key_values[:, :key_width].astype(jnp.float32)
    grad_values = grad_key_values[:, key_width:]
    grad_queries = (
        rotate(grad_queries_rot, cosine, -sine_table)
        .astype(jnp.bfloat16)
        .reshape(row_count, query_width)
    )
    grad_keys = (
        rotate(grad_keys_sum.reshape(row_count, shared_heads, HD), cosine, -sine_table)
        .astype(jnp.bfloat16)
        .reshape(row_count, key_width)
    )
    grad_qkv = jnp.concatenate([grad_queries, grad_keys, grad_values], axis=1)
    qkv_grad = inner_rows(normed_first, grad_qkv).astype(jnp.bfloat16)
    bias_grad = jnp.sum(grad_qkv.astype(jnp.float32), axis=0)
    grad_first = times_transposed(grad_qkv, qkv_matrix)
    first_gain_grad = jnp.sum(grad_first * inputs * scale_first, axis=0)
    tokens_grad = (
        (grad_hidden + norm_back(grad_first, inputs, scale_first, gain_first))
        .astype(jnp.bfloat16)
        .reshape(tokens.shape)
    )
    small_grad = jnp.concatenate(
        [
            piece.astype(jnp.bfloat16).reshape(shards, -1)
            for piece in (
                first_gain_grad,
                second_gain_grad,
                bias_grad[:query_width],
                bias_grad[query_width : query_width + key_width],
                bias_grad[query_width + key_width :],
            )
        ],
        axis=1,
    )
    extra_rows = small.shape[0]
    small_grad = jnp.pad(
        small_grad, ((0, 0), (0, extra_rows * qkv_width - small_grad.shape[1]))
    ).reshape(shards, extra_rows, qkv_width)
    first_owned = lax.psum_scatter(
        jnp.concatenate([qkv_grad.reshape(shards, own_rows, qkv_width), small_grad], axis=1),
        "shard",
        scatter_dimension=0,
        tiled=False,
    )
    first_owned, out_owned = lax.psum((first_owned, later_owned[:, :model_width]), "rep")
    first_owned = first_owned.astype(jnp.float32)
    hidden_set = lax.all_gather(later_owned[:, model_width:], "rep", axis=0, tiled=False)
    down_set = lax.all_gather(down_owned, "rep", axis=0, tiled=True)

    def spread_columns(parts):
        grouped = parts.reshape(reps, own_rows, shards, part_hidden)
        return grouped.transpose(1, 2, 0, 3).reshape(own_rows, hidden_width).astype(jnp.float32)

    small_owned = first_owned[own_rows:].reshape(-1)
    small_outs = [small_owned[starts[i] : starts[i] + sizes[i]] for i in range(len(sizes))]
    return (
        output,
        tokens_grad,
        small_outs[0],
        first_owned[:own_rows, :query_width],
        small_outs[2],
        first_owned[:own_rows, query_width : query_width + key_width],
        small_outs[3],
        first_owned[:own_rows, query_width + key_width :],
        small_outs[4],
        out_owned.astype(jnp.float32),
        small_outs[1],
        spread_columns(hidden_set[:, :, :slice_width]),
        spread_columns(hidden_set[:, :, padded_width:]),
        down_set.astype(jnp.float32),
    )


def solution(mesh):
    placed = (
        P("rep", "shard", None),
        P("rep", "shard"),
        P("shard"),
        P("shard", None),
        P("shard"),
        P("shard", None),
        P("shard"),
        P("shard", None),
        P("shard"),
        P("shard", None),
        P("shard"),
        P("shard", None),
        P("shard", None),
        P("shard", None),
        P("rep", "shard", None),
    )
    return jax.shard_map(
        functools.partial(on_device, reps=mesh.shape["rep"], shards=mesh.shape["shard"]),
        mesh=mesh,
        in_specs=placed,
        out_specs=(
            P("rep", "shard", None),
            P("rep", "shard", None),
            P("shard"),
            P("shard", None),
            P("shard"),
            P("shard", None),
            P("shard"),
            P("shard", None),
            P("shard"),
            P("shard", None),
            P("shard"),
            P("shard", None),
            P("shard", None),
            P("shard", None),
        ),
        check_vma=False,
    )
```

time: 1730 us -> 1080 us (0.62)
  waiting for transfers between devices: 1160 us -> 618 us
  blocking collectives: 143 us -> 0 us
  local copies, waits for them, and re-layouts: 33.2 us -> 81.2 us
  matrix products: 271 us -> 242 us
  other arithmetic: 94.2 us -> 113 us
    reduce_scatter x9 -> x3, waiting for transfers between devices: 710 us -> 73.3 us  [the longest x1 41.5 us: on_device(): lax.psum_scatter(output_part.astype(jnp.bfloat16), 'rep', scatter_dimensi...]
    unnamed x17 -> x18, waiting for transfers between devices: 3.17 us -> 255 us
    all_gather x7 -> x8, waiting for transfers between devices: 388 us -> 258 us  [the longest x1 56.7 us: on_device(): key_values = lax.all_gather(key_values, 'shard', axis=1, tiled=True)]
    all_gather x3 -> x0, blocking collectives: 88.4 us -> none  [the longest x1 31.3 us: on_device(): lax.all_gather(key_weight, 'shard', axis=0, tiled=True)]
    unnamed x2 -> x0, blocking collectives: 43.1 us -> none
    psum x1, waiting for transfers between devices: 63.9 us -> 31.5 us  [on_device(): lax.psum((first_owned, later_owned[:, :model_width]), 'rep')]
    concatenate x0 -> x6, other arithmetic: none -> 23.7 us  [the longest x1 15.3 us: on_device(): jnp.concatenate([out_grad, widen(gate_grad), up_grad], axis=1)]
    slice x0 -> x18, local copies, waits for them, and re-layouts: none -> 18.1 us  [the longest x2 3.53 us: on_device(): linear[:, :query_width + key_width]]
  transfers between devices with their start and end apart: 17 -> 15, of which waited for: 14 -> 14; matrix products, arithmetic and copies ran while one was open for 13% -> 20% of each run, Pallas kernels for 0% -> 0%
where the time goes in v1:
time: 1080 us; the launch traced here: 1070 us
  waiting for transfers between devices  618 us (57%)
  matrix products  242 us (22%)
  other arithmetic  113 us (10%)
  local copies, waits for them, and re-layouts  81.2 us (8%)
  between operations  14.8 us (1%)
    unnamed x18, waiting for transfers between devices  255 us
    all_gather x1, waiting for transfers between devices, on_device(): key_values = lax.all_gather(key_values, 'shard', axis=1, tiled=True)  56.7 us
    convert_element_type x1, other arithmetic, attend_back(): grad_scores = (probs_full * (grad_probs - row_delta)).astype(jnp.bfloat16)  46.6 us
    dot_general x5, matrix products, times_transposed(): lax.dot_general(left_side, right_side, (((1,), (1,)), ((), ())), preferre...  45.1 us
    all_gather x1, waiting for transfers between devices, on_device(): lax.all_gather(jnp.concatenate([qkv_part, small], axis=0), 'shard', axis=...  44.3 us
    reduce_scatter x1, waiting for transfers between devices, on_device(): lax.psum_scatter(output_part.astype(jnp.bfloat16), 'rep', scatter_dimensi...  41.5 us
    dot_general x1, matrix products, attend_back(): jnp.einsum('bqkgd,bskd->bkgqs', grad_block, value_block, preferred_elemen...  38 us
    all_gather x1, waiting for transfers between devices, on_device(): down_matrix = lax.all_gather(down_part, 'shard', axis=0, tiled=True)  33 us
  transfers between devices with their start and end apart: 15, of which 14 were waited for; matrix products, arithmetic and copies ran while one was open for 20% of the time, Pallas kernels for 0%

profile of v1, /device:TPU:0, one launch (start us, length us, event | category | flops | bytes accessed | tf_op | source)
XLA Modules:
  0.0 1070.7 jit_solution(8304934045091872229)
XLA Ops:
  22.3 44.3 %all-gather.23.cloned.1.call-done = bf16[960,1152]{1,0:T(8,128)(2,1)} async-done(((bf16[120,1152]{1,0:T(8,128)(2,1)}), bf16[960,1152]{1,0:T(8,128)(2,1)}) %all-gather.23.cloned.1.call-update) | async-done | bytes 2211856 | tf_op jit(solution)/shard_map/all_gather | solution.py:164
  86.7 56.7 %all-gather.11.cloned.1.call-done = bf16[2,2048,256]{1,0,2:T(2,128)(2,1)} async-done(((bf16[2,256,256]{1,0,2:T(2,128)(2,1)}), bf16[2,2048,256]{1,0,2:T(2,128)(2,1)}) %all-gather.11.cloned.1.call-update) | async-done | bytes 2097168 | tf_op jit(solution)/shard_map/all_gather | solution.py:217
  146.8 21.3 %fusion.9 = (f32[2,2,7,256]{3,2,1,0:T(8,128)S(1)}, f32[2,2,2048,256,7]{3,2,4,1,0:T(8,128)}) fusion(pred[2,256,2048]{1,2,0:T(8,128)(4,1)S(1)} %compare_and_fusion, bf16[2,2048,2,64,1]{1,3,4,2,0:T(8,128)(2,1)S(1)} %bitcast.186, bf16[2,256,2,7,64]{1,0,4,3,2:T(2,128)(2,1)S(1)} %squeeze.37), kind=kOutput, calls=%fused_computation.14 | convolution fusion | flops 1923081216 | bytes 61763584 | tf_op jit(solution)/shard_map/while/body/eval_jaxpr/bqkgd,bskd->bkgqs/dot_general | solution.py:57
  168.2 19.1 %fusion.3 = f32[2,2,7,256]{3,2,1,0:T(8,128)S(1)} fusion(f32[2,2,7,256]{3,2,1,0:T(8,128)S(1)} %get-tuple-element.172, f32[2,2,2048,256,7]{3,2,4,1,0:T(8,128)} %get-tuple-element.173, pred[2,256,2048]{1,2,0:T(8,128)(4,1)S(1)} %compare_and_fusion), kind=kLoop, calls=%fused_computation.9 | loop fusion | flops 58713088 | bytes 59826176 | tf_op jit(solution)/shard_map/while/body/eval_jaxpr/reduce_sum | solution.py:68
  187.3 22.8 %fusion.56 = bf16[2,256,2,7,64]{1,4,3,2,0:T(8,128)(2,1)S(1)} fusion(bf16[2,2048,2,64,1]{1,3,4,2,0:T(8,128)(2,1)S(1)} %bitcast.189, f32[2,2,7,256]{3,2,1,0:T(8,128)S(1)} %fusion.3, f32[2,2,7,256]{3,2,1,0:T(8,128)S(1)} %get-tuple-element.172, f32[2,2,2048,256,7]{3,2,4,1,0:T(8,128)} %get-tuple-element.173, pred[2,256,2048]{1,2,0:T(8,128)(4,1)S(1)} %compare_and_fusion), kind=kOutput, calls=%fused_computation.91 | convolution fusion | flops 1952907264 | bytes 61792256 | tf_op jit(solution)/shard_map/while/body/eval_jaxpr/bkgqs,bskd->bqkgd/dot_general | solution.py:70
  212.2 30.0 %all-gather.13.cloned.1.call-done = bf16[896,3392]{1,0:T(8,128)(2,1)} async-done(((bf16[112,3392]{1,0:T(8,128)(2,1)}), bf16[896,3392]{1,0:T(8,128)(2,1)}) %all-gather.13.cloned.1.call-update) | async-done | bytes 6078480 | tf_op jit(solution)/shard_map/all_gather | solution.py:218
  248.2 28.4 %all-gather.15.cloned.1.call-done = bf16[2048,896]{1,0:T(8,128)(2,1)} async-done(((bf16[512,896]{1,0:T(8,128)(2,1)}), bf16[2048,896]{1,0:T(8,128)(2,1)}) %all-gather.15.cloned.1.call-update) | async-done | bytes 3670032 | tf_op jit(solution)/shard_map/all_gather | solution.py:235
  276.6 10.2 fusion.26
  286.8 9.7 fusion.30
  296.5 33.0 %all-gather.17.cloned.1.call-done = bf16[1216,896]{1,0:T(8,128)(2,1)} async-done(((bf16[152,896]{1,0:T(8,128)(2,1)}), bf16[1216,896]{1,0:T(8,128)(2,1)}) %all-gather.17.cloned.1.call-update) | async-done | bytes 2179088 | tf_op jit(solution)/shard_map/all_gather | solution.py:219
  329.4 31.5 %all-gather.19.cloned.1.call-done = bf16[2048,896]{1,0:T(8,128)(2,1)} async-done(((bf16[512,896]{1,0:T(8,128)(2,1)}), bf16[2048,896]{1,0:T(8,128)(2,1)}) %all-gather.19.cloned.1.call-update) | async-done | bytes 3670032 | tf_op jit(solution)/shard_map/all_gather | solution.py:221
  360.9 17.5 %multiply_convert_fusion = (bf16[2048,1216]{0,1:T(8,128)(2,1)S(1)}, bf16[2048,1216]{0,1:T(8,128)(2,1)}, bf16[2048,1216]{0,1:T(8,128)(2,1)}) fusion(f32[2048,1216]{0,1:T(8,128)} %fusion.30, f32[2048,1216]{0,1:T(8,128)} %fusion.26, bf16[2048,896]{1,0:T(8,128)(2,1)} %all-gather.19.cloned.1.call-done, bf16[1216,896]{1,0:T(8,128)(2,1)} %all-gather.17.cloned.1.call-done), kind=kOutput, calls=%fused_computation.19 | convolution fusion | flops 4500094976 | bytes 40714240 | tf_op jit(solution)/shard_map/dot_general | solution.py:43
  378.4 10.1 fusion.28
  388.5 8.9 add_convert_fusion
  397.5 9.5 convolution_convert_fusion.4
  407.0 31.8 %reduce-scatter.15.cloned.1.call-done = bf16[512,896]{1,0:T(8,128)(2,1)} async-done(((bf16[2048,896]{1,0:T(8,128)(2,1)}), bf16[512,896]{1,0:T(8,128)(2,1)}) %reduce-scatter.15.cloned.1.call-update) | async-done | bytes 917520 | tf_op jit(solution)/shard_map/reduce_scatter | solution.py:247
  441.3 41.5 %reduce-scatter.13.cloned.1.call-done = bf16[512,896]{1,0:T(8,128)(2,1)} async-done(((bf16[2048,896]{1,0:T(8,128)(2,1)}), bf16[512,896]{1,0:T(8,128)(2,1)}) %reduce-scatter.13.cloned.1.call-update) | async-done | bytes 917520 | tf_op jit(solution)/shard_map/reduce_scatter | solution.py:283
  496.5 23.2 %fusion.20 = bf16[2,2,64,2048]{3,2,1,0:T(8,128)(2,1)} fusion(bf16[2,256,2,7,64]{1,4,3,2,0:T(8,128)(2,1)} %copy.110, f32[2,2,7,256]{3,2,1,0:T(8,128)S(1)} %log_add_fusion, f32[2,2,2048,256,7]{3,2,4,1,0:T(8,128)} %get-tuple-element.173, pred[2,256,2048]{1,2,0:T(8,128)(4,1)S(1)} %compare_and_fusion), kind=kOutput, calls=%fused_computation.41 | convolution fusion | flops 1938292736 | bytes 61763584 | tf_op jit(solution)/shard_map/while/body/eval_jaxpr/bkgqs,bqkgd->bskd/dot_general | solution.py:89
  519.7 38.0 %fusion = (f32[2,2,7,256]{3,2,1,0:T(8,128)S(1)}, f32[2,2,2048,256,7]{3,2,4,1,0:T(8,128)}) fusion(f32[2,2,7,256]{3,2,1,0:T(8,128)S(1)} %log_add_fusion, f32[2,2,2048,256,7]{3,2,4,1,0:T(8,128)} %get-tuple-element.173, pred[2,256,2048]{1,2,0:T(8,128)(4,1)S(1)} %compare_and_fusion, bf16[2,2048,2,64,1]{1,3,4,2,0:T(8,128)(2,1)S(1)} %bitcast.190, ...), kind=kOutput, calls=%fused_computation.2 | convolution fusion | flops 1952441344 | bytes 120512512 | tf_op jit(solution)/shard_map/while/body/eval_jaxpr/bqkgd,bskd->bkgqs/dot_general | solution.py:78
  559.3 46.6 %fusion.2 = bf16[2,2,7,256,2048]{3,4,2,1,0:T(8,128)(2,1)} fusion(f32[2,2,2048,256,7]{3,2,4,1,0:T(8,128)} %get-tuple-element.177, f32[2,2,7,256]{3,2,1,0:T(8,128)S(1)} %get-tuple-element.176, f32[2,2,7,256]{3,2,1,0:T(8,128)S(1)} %log_add_fusion, f32[2,2,2048,256,7]{3,2,4,1,0:T(8,128)} %get-tuple-element.173, pred[2,256,2048]{1,2,0:T(8,128)(4,1)S(1)} %compare_and_fusion), kind=kLoop, calls=%fused_computation.4 | loop fusion | flops 88080384 | bytes 147906560 | tf_op jit(solution)/shard_map/while/body/eval_jaxpr/convert_element_type | solution.py:82
  605.8 14.9 %fusion.19 = bf16[2,2,64,2048]{3,2,1,0:T(8,128)(2,1)S(1)} fusion(bf16[2,2,7,256,2048]{3,4,2,1,0:T(8,128)(2,1)} %fusion.2, bf16[2,256,2,7,64]{1,0,4,3,2:T(2,128)(2,1)S(1)} %copy-done.5), kind=kOutput, calls=%fused_computation.40 | convolution fusion | flops 1880096768 | bytes 31326208 | tf_op jit(solution)/shard_map/while/body/eval_jaxpr/bkgqs,bqkgd->bskd/dot_general | solution.py:86
  625.1 9.3 convolution_convert_fusion.2
  634.5 8.4 convolution_convert_fusion
  651.6 15.3 %fusion.13 = bf16[896,3392]{0,1:T(8,128)(2,1)} fusion(bf16[896,1216]{0,1:T(8,128)(2,1)S(1)} %convolution_convert_fusion.1, bf16[896,1216]{0,1:T(8,128)(2,1)S(1)} %convolution_convert_fusion, bf16[896,896]{0,1:T(8,128)(2,1)S(1)} %convolution_convert_fusion.5), kind=kLoop, calls=%fused_computation.25 | loop fusion | flops 30392320 | bytes 12042240 | tf_op jit(solution)/shard_map/concatenate | solution.py:261
  666.8 9.2 copy.137
  677.3 12.3 %multiply_bitcast_fusion = f32[2,256,2,7,64]{1,4,3,2,0:T(8,128)S(1)} fusion(bf16[2,2048,2,64,1]{1,3,4,2,0:T(8,128)(2,1)S(1)} %bitcast.187, bf16[2,2,7,256,2048]{3,4,2,1,0:T(8,128)(2,1)} %fusion.2), kind=kOutput, calls=%fused_computation.80 | convolution fusion | flops 1879506944 | bytes 32243712 | tf_op jit(solution)/shard_map/while/body/eval_jaxpr/bkgqs,bskd->bqkgd/dot_general | solution.py:83
  707.1 62.8 %reduce-scatter.23.cloned.1.call-done = bf16[152,896]{1,0:T(8,128)(2,1)} async-done(((bf16[1216,896]{1,0:T(8,128)(2,1)}), bf16[152,896]{1,0:T(8,128)(2,1)}) %reduce-scatter.23.cloned.1.call-update) | async-done | bytes 272400
  770.0 121.3 %reduce-scatter.19.cloned.1.call-done = bf16[112,3392]{1,0:T(8,128)(2,1)} async-done(((bf16[896,3392]{1,0:T(8,128)(2,1)}), bf16[112,3392]{1,0:T(8,128)(2,1)}) %reduce-scatter.19.cloned.1.call-update) | async-done | bytes 759824
  893.1 69.8 %reduce-scatter.21.cloned.1.call-done = bf16[1,120,1152]{2,1,0:T(8,128)(2,1)} async-done(((bf16[8,120,1152]{2,1,0:T(8,128)(2,1)}), bf16[1,120,1152]{2,1,0:T(8,128)(2,1)}) %reduce-scatter.21.cloned.1.call-update) | async-done | bytes 276496
  965.0 15.2 %all-gather.21.cloned.1.call-done = bf16[608,896]{1,0:T(8,128)(2,1)} async-done(((bf16[152,896]{1,0:T(8,128)(2,1)}), bf16[608,896]{1,0:T(8,128)(2,1)}) %all-gather.21.cloned.1.call-update) | async-done | bytes 1089552 | tf_op jit(solution)/shard_map/all_gather | solution.py:349
  984.6 31.5 %all-reduce.9.cloned.1.call-done = (bf16[120,1152]{1,0:T(8,128)(2,1)}, bf16[112,896]{0,1:T(8,128)(2,1)}) async-done(((bf16[120,1152]{1,0:T(8,128)(2,1)}, bf16[112,896]{0,1:T(8,128)(2,1)}), (bf16[120,1152]{1,0:T(8,128)(2,1)}, bf16[112,896]{0,1:T(8,128)(2,1)})) %all-reduce.9.cloned.1.call-update) | async-done | bytes 477200 | tf_op jit(solution)/shard_map/psum | solution.py:346
  1023.0 19.3 %all-gather.25.cloned.1.call-done = bf16[448,2496]{1,0:T(8,128)(2,1)} async-done(((bf16[112,2496]{1,0:T(8,128)(2,1)}), bf16[448,2496]{1,0:T(8,128)(2,1)}) %all-gather.25.cloned.1.call-update) | async-done | bytes 2236432 | tf_op jit(solution)/shard_map/all_gather | solution.py:348
  (198 shorter events, 132.6 us)
Async XLA Ops:
  7.2 11.4 %copy-start = (bf16[608,896]{1,0:T(8,128)(2,1)S(1)}, bf16[608,896]{1,0:T(8,128)(2,1)}, u32[]{:S(2)}) copy-start(bf16[608,896]{1,0:T(8,128)(2,1)} %param.28) | copy-start | bytes 3268612
  7.2 59.4 %all-gather.23.cloned.1.call-start = ((), (), s32[]{:S(2)}) async-start(), calls=%async_computation.15 | async-start | bytes 2488320 | tf_op jit(solution)/shard_map/all_gather | solution.py:164
  13.2 130.2 %all-gather.11.cloned.1.call-start = ((), (), s32[]{:S(2)}) async-start(), calls=%async_computation.6 | async-start | bytes 2359296 | tf_op jit(solution)/shard_map/all_gather | solution.py:217
  16.1 4.3 copy-start.6
  71.2 3.4 copy-start.19
  82.0 160.3 %all-gather.13.cloned.1.call-start = ((), (), s32[]{:S(2)}) async-start(), calls=%async_computation.7 | async-start | bytes 6967296 | tf_op jit(solution)/shard_map/all_gather | solution.py:218
  82.8 64.0 %copy-start.4 = (bf16[2,256,2,7,64]{1,0,4,3,2:T(2,128)(2,1)}, bf16[2,256,2,7,64]{1,0,4,3,2:T(2,128)(2,1)S(1)}, u32[]{:S(2)}) copy-start(bf16[2,256,2,7,64]{1,0,4,3,2:T(2,128)(2,1)S(1)} %squeeze.37) | copy-start | bytes 2752516
  86.4 190.1 %all-gather.15.cloned.1.call-start = ((), (), s32[]{:S(2)}) async-start(), calls=%async_computation.8 | async-start | bytes 4587520 | tf_op jit(solution)/shard_map/all_gather | solution.py:235
  146.4 21.7 %copy-start.2 = (bf16[2,2048,128]{1,2,0:T(8,128)(2,1)}, bf16[2,2048,128]{1,2,0:T(8,128)(2,1)S(1)}, u32[]{:S(2)}) copy-start(bf16[2,2048,128]{1,2,0:T(8,128)(2,1)S(1)} %copy.104) | copy-start | bytes 3145732
  146.8 40.5 %copy-start.12 = (bf16[2,2048,128]{1,2,0:T(8,128)(2,1)}, bf16[2,2048,128]{1,2,0:T(8,128)(2,1)S(1)}, u32[]{:S(2)}) copy-start(bf16[2,2048,128]{1,2,0:T(8,128)(2,1)S(1)} %copy.103) | copy-start | bytes 3145732
  246.7 82.7 %all-gather.17.cloned.1.call-start = ((), (), s32[]{:S(2)}) async-start(), calls=%async_computation.9 | async-start | bytes 2451456 | tf_op jit(solution)/shard_map/all_gather | solution.py:219
  247.3 113.5 %all-gather.19.cloned.1.call-start = ((), (), s32[]{:S(2)}) async-start(), calls=%async_computation.11 | async-start | bytes 4587520 | tf_op jit(solution)/shard_map/all_gather | solution.py:221
  247.9 190.9 %reduce-scatter.15.cloned.1.call-start = ((), (), s32[]{:S(2)}) async-start(), calls=%async_computation.12 | async-start | bytes 4587520 | tf_op jit(solution)/shard_map/reduce_scatter | solution.py:247
  276.6 10.2 copy-start.24
  378.4 10.1 copy-start.26
  397.4 85.4 %reduce-scatter.13.cloned.1.call-start = ((), (), s32[]{:S(2)}) async-start(), calls=%async_computation.10 | async-start | bytes 4587520 | tf_op jit(solution)/shard_map/reduce_scatter | solution.py:283
  407.0 288.7 %reduce-scatter.17.cloned.1.call-start = ((), (), s32[]{:S(2)}) async-start(), calls=%async_computation.13 | async-start | bytes 2359296 | tf_op jit(solution)/shard_map/reduce_scatter | solution.py:298
  496.5 23.2 %copy-start.11 = (bf16[2,256,2,7,64]{1,4,3,2,0:T(8,128)(2,1)S(1)}, bf16[2,256,2,7,64]{1,4,3,2,0:T(8,128)(2,1)}, u32[]{:S(2)}) copy-start(bf16[2,256,2,7,64]{1,4,3,2,0:T(8,128)(2,1)} %copy.110) | copy-start | bytes 2752516
  496.5 23.2 %copy-start.13 = (bf16[2,2048,128]{1,2,0:T(8,128)(2,1)S(1)}, bf16[2,2048,128]{1,2,0:T(8,128)(2,1)}, u32[]{:S(2)}) copy-start(bf16[2,2048,128]{1,2,0:T(8,128)(2,1)} %copy-done.12) | copy-start | bytes 3145732
  559.3 46.6 %copy-start.5 = (bf16[2,256,2,7,64]{1,0,4,3,2:T(2,128)(2,1)S(1)}, bf16[2,256,2,7,64]{1,0,4,3,2:T(2,128)(2,1)}, u32[]{:S(2)}) copy-start(bf16[2,256,2,7,64]{1,0,4,3,2:T(2,128)(2,1)} %copy-done.4) | copy-start | bytes 2752516
  625.1 144.9 %reduce-scatter.23.cloned.1.call-start = ((), (), s32[]{:S(2)}) async-start(), calls=%async_computation.19 | async-start | bytes 2451456
  634.4 256.9 %reduce-scatter.19.cloned.1.call-start = ((), (), s32[]{:S(2)}) async-start(), calls=%async_computation.17 | async-start | bytes 6967296
  634.5 8.5 copy-start.25
  642.9 7.4 copy-start.9
  642.9 7.4 copy-start.17
  676.1 286.8 %reduce-scatter.21.cloned.1.call-start = ((), (), s32[]{:S(2)}) async-start(), calls=%async_computation.18 | async-start | bytes 2488320
  707.1 273.2 %all-gather.21.cloned.1.call-start = ((), (), s32[]{:S(2)}) async-start(), calls=%async_computation.14 | async-start | bytes 1361920 | tf_op jit(solution)/shard_map/all_gather | solution.py:349
  770.0 246.1 %all-reduce.9.cloned.1.call-start = ((), (), s32[]{:S(2)}) async-start(), calls=%async_computation.20 | async-start | bytes 1011712 | tf_op jit(solution)/shard_map/psum | solution.py:346
  962.9 20.2 %copy-start.10 = (f32[512,896]{1,0:T(8,128)S(1)}, f32[512,896]{1,0:T(8,128)}, u32[]{:S(2)}) copy-start(f32[512,896]{1,0:T(8,128)} %copy-done.8) | copy-start | bytes 5505028
  962.9 79.3 %all-gather.25.cloned.1.call-start = ((), (), s32[]{:S(2)}) async-start(), calls=%async_computation.16 | async-start | bytes 2867200 | tf_op jit(solution)/shard_map/all_gather | solution.py:348
  980.3 2.9 copy-start.14
  1057.4 6.6 copy-start.1
  (10 other events, 15.8 us)
Sparse Core Ops, SparseCore 0:
  13.3 53.2 all-gather.22
  82.1 61.2 all-gather.10
  146.1 96.0 all-gather.12
  246.9 29.6 all-gather.14
  279.2 50.1 all-gather.16
  330.8 29.9 all-gather.18
  397.5 41.2 reduce-scatter.14
  441.5 41.2 reduce-scatter.12
  625.2 67.6 reduce-scatter.16
  696.7 73.1 reduce-scatter.22
  774.1 117.1 reduce-scatter.18
  895.2 67.6 reduce-scatter.20
  964.4 15.7 all-gather.20
  983.1 32.9 all-reduce.8
  1018.1 24.0 all-gather.24

commit v2 on v1

--- a/solution.py
+++ b/solution.py
@@ -99,6 +99,57 @@
     flat = jnp.concatenate(pieces)
     rows = -(-flat.shape[0] // (8 * width)) * 8
     return jnp.pad(flat, (0, rows * width - flat.shape[0])).reshape(rows, width)
+
+
+def partner_swap(values, bit, reps):
+    return lax.ppermute(values, "rep", [(i, i ^ bit) for i in range(reps)])
+
+
+def rep_bits(reps):
+    return [1 << i for i in range(reps.bit_length() - 1)]
+
+
+def rep_places(reps):
+    places = [0]
+    for bit in reversed(rep_bits(reps)):
+        places = places + [place ^ bit for place in places]
+    return places
+
+
+def rep_gather(values, reps):
+    for bit in reversed(rep_bits(reps)):
+        values = jnp.concatenate([values, partner_swap(values, bit, reps)], axis=0)
+    return values
+
+
+def rep_scatter(values, reps):
+    for bit in rep_bits(reps):
+        half = values.shape[0] // 2
+        received = partner_swap(values[half:].astype(jnp.bfloat16), bit, reps)
+        values = values[:half].astype(jnp.float32) + received.astype(jnp.float32)
+    return values.astype(jnp.float32)
+
+
+def rep_sum(values, reps):
+    for bit in rep_bits(reps):
+        sent = values.astype(jnp.bfloat16)
+        received = partner_swap(sent, bit, reps)
+        values = sent.astype(jnp.float32) + received.astype(jnp.float32)
+    return values
+
+
+def rep_ordered(values, reps, rep_index):
+    gathered = rep_gather(values[None], reps)
+    where_is = [0] * reps
+    for spot, place in enumerate(rep_places(reps)):
+        where_is[place] = spot
+    table = jnp.asarray(where_is, dtype=jnp.int32)
+    return jnp.stack(
+        [
+            lax.dynamic_index_in_dim(gathered, table[rep_index ^ i], 0, keepdims=False)
+            for i in range(reps)
+        ]
+    )
 
 
 def on_device(
@@ -211,14 +262,14 @@
         [out_weight, widen(pick_columns(gate_weight)), pick_columns(up_weight)], axis=1
     )
     down_part = lax.dynamic_slice_in_dim(down_weight, rep_index * part_hidden, part_hidden, 0)
-    key_values, later_part, down_part, cotangent = lax.optimization_barrier(
-        (key_values, later_part, down_part, cotangent)
+    key_values, later_part, down_part = lax.optimization_barrier(
+        (key_values, later_part, down_part)
     )
     key_values = lax.all_gather(key_values, "shard", axis=1, tiled=True)
     later_set = lax.all_gather(later_part, "shard", axis=0, tiled=True)
     down_matrix = lax.all_gather(down_part, "shard", axis=0, tiled=True)
     grad_output = cotangent.reshape(row_count, model_width)
-    grad_output_all = lax.all_gather(grad_output, "rep", axis=0, tiled=True)
+    grad_output_all = rep_gather(grad_output, reps)
     output_matrix = later_set[:, :model_width]
     gate_matrix = later_set[:, model_width : model_width + slice_width]
     up_matrix = later_set[:, model_width + padded_width :]
@@ -232,7 +283,7 @@
     hidden = inputs + jnp.dot(mixed_heads, output_matrix, preferred_element_type=jnp.float32)
     scale_second = rms_scale(hidden)
     normed_second = (hidden * scale_second * gain_second.astype(jnp.float32)).astype(jnp.bfloat16)
-    normed_all = lax.all_gather(normed_second, "rep", axis=0, tiled=True)
+    normed_all = rep_gather(normed_second, reps)
     gate_linear = jnp.dot(normed_all, gate_matrix, preferred_element_type=jnp.float32)
     up_linear = jnp.dot(normed_all, up_matrix, preferred_element_type=jnp.float32)
     sigmoid_gate = jax.nn.sigmoid(gate_linear)
@@ -244,26 +295,23 @@
     grad_normed_part = (
         times_transposed(grad_gate, gate_matrix) + times_transposed(grad_up, up_matrix)
     ).astype(jnp.bfloat16)
-    grad_normed = lax.psum_scatter(
-        grad_normed_part, "rep", scatter_dimension=0, tiled=True
-    ).astype(jnp.float32)
+    grad_normed = rep_scatter(grad_normed_part, reps)
     down_grad = inner_rows(activation, grad_output_all).astype(jnp.bfloat16)
     gate_grad = inner_rows(normed_all, grad_gate).astype(jnp.bfloat16)
     up_grad = inner_rows(normed_all, grad_up).astype(jnp.bfloat16)
-    down_owned = lax.psum_scatter(down_grad, "shard", scatter_dimension=0, tiled=True)
     second_gain_grad = jnp.sum(grad_normed * hidden * scale_second, axis=0)
     grad_hidden = grad_output.astype(jnp.float32) + norm_back(
         grad_normed, hidden, scale_second, gain_second
     )
     grad_branch = grad_hidden.astype(jnp.bfloat16)
     out_grad = inner_rows(mixed_heads, grad_branch).astype(jnp.bfloat16)
-    later_owned = lax.psum_scatter(
-        jnp.concatenate([out_grad, widen(gate_grad), up_grad], axis=1),
-        "shard",
-        scatter_dimension=0,
-        tiled=True,
-    )
+    later_grad = jnp.concatenate([out_grad, widen(gate_grad), up_grad], axis=1)
     grad_mixed = times_transposed(grad_branch, output_matrix).astype(jnp.bfloat16)
+    grad_mixed, later_grad, down_grad = lax.optimization_barrier(
+        (grad_mixed, later_grad, down_grad)
+    )
+    down_owned = lax.psum_scatter(down_grad, "shard", scatter_dimension=0, tiled=True)
+    later_owned = lax.psum_scatter(later_grad, "shard", scatter_dimension=0, tiled=True)
     grad_mixed = grad_mixed.reshape(sequences, local_tokens, shared_heads, group_size, HD)
     grad_query_blocks, grad_key_blocks, grad_value_blocks = lax.map(
         attend_back,
@@ -280,9 +328,7 @@
     output = (
         (
             hidden
-            + lax.psum_scatter(
-                output_part.astype(jnp.bfloat16), "rep", scatter_dimension=0, tiled=True
-            ).astype(jnp.float32)
+            + rep_scatter(output_part.astype(jnp.bfloat16), reps)
         )
         .astype(jnp.bfloat16)
         .reshape(tokens.shape)
@@ -343,10 +389,10 @@
         scatter_dimension=0,
         tiled=False,
     )
-    first_owned, out_owned = lax.psum((first_owned, later_owned[:, :model_width]), "rep")
-    first_owned = first_owned.astype(jnp.float32)
-    hidden_set = lax.all_gather(later_owned[:, model_width:], "rep", axis=0, tiled=False)
-    down_set = lax.all_gather(down_owned, "rep", axis=0, tiled=True)
+    first_owned = rep_sum(first_owned, reps)
+    out_owned = rep_sum(later_owned[:, :model_width], reps)
+    hidden_set = rep_ordered(later_owned[:, model_width:], reps, rep_index)
+    down_set = rep_ordered(down_owned, reps, rep_index).reshape(own_hidden, model_width)
 
     def spread_columns(parts):
         grouped = parts.reshape(reps, own_rows, shards, part_hidden)

time: 1080 us -> 972 us (0.900)
  waiting for transfers between devices: 618 us -> 497 us
  starting transfers between devices: 0.99 us -> 14.5 us
    all_gather x4 -> x0, waiting for transfers between devices: 94.4 us -> none  [the longest x1 31.5 us: on_device(): grad_output_all = lax.all_gather(grad_output, 'rep', axis=0, tiled=True)]
    ppermute x0 -> x16, waiting for transfers between devices: none -> 87.7 us  [partner_swap(): return lax.ppermute(values, 'rep', [(i, i ^ bit) for i in range(reps)])]
    reduce_scatter x2 -> x0, waiting for transfers between devices: 73.3 us -> none  [the longest x1 41.5 us: on_device(): lax.psum_scatter(output_part.astype(jnp.bfloat16), 'rep', scatter_dimensi...]
    reduce_scatter x1, waiting for transfers between devices: 0.02 us -> 47.2 us  [on_device(): lax.psum_scatter(grad_key_values, 'shard', scatter_dimension=1, tiled=True)]
    all_gather x1, waiting for transfers between devices: 33 us -> 0.01 us  [on_device(): down_matrix = lax.all_gather(down_part, 'shard', axis=0, tiled=True)]
    psum x1 -> x0, waiting for transfers between devices: 31.5 us -> none  [on_device(): lax.psum((first_owned, later_owned[:, :model_width]), 'rep')]
    unnamed x18 -> x11, waiting for transfers between devices: 255 us -> 231 us
    ppermute x0 -> x16, starting transfers between devices: none -> 13.4 us  [partner_swap(): return lax.ppermute(values, 'rep', [(i, i ^ bit) for i in range(reps)])]
  transfers between devices with their start and end apart: 15 -> 24, of which waited for: 14 -> 14; matrix products, arithmetic and copies ran while one was open for 20% -> 21% of each run, Pallas kernels for 0% -> 0%
where the time goes in v2:
time: 972 us; the launch traced here: 965 us
  waiting for transfers between devices  497 us (51%)
  matrix products  237 us (24%)
  other arithmetic  117 us (12%)
  local copies, waits for them, and re-layouts  76.8 us (8%)
  between operations  23 us (2%)
  starting transfers between devices  14.5 us (1%)
    unnamed x11, waiting for transfers between devices  231 us
    ppermute x16, waiting for transfers between devices, partner_swap(): return lax.ppermute(values, 'rep', [(i, i ^ bit) for i in range(reps)])  87.7 us
    all_gather x1, waiting for transfers between devices, on_device(): key_values = lax.all_gather(key_values, 'shard', axis=1, tiled=True)  56.4 us
    reduce_scatter x1, waiting for transfers between devices, on_device(): lax.psum_scatter(grad_key_values, 'shard', scatter_dimension=1, tiled=True)  47.2 us
    convert_element_type x1, other arithmetic, attend_back(): grad_scores = (probs_full * (grad_probs - row_delta)).astype(jnp.bfloat16)  46.5 us
    all_gather x1, waiting for transfers between devices, on_device(): lax.all_gather(jnp.concatenate([qkv_part, small], axis=0), 'shard', axis=...  44.3 us
    dot_general x5, matrix products, times_transposed(): lax.dot_general(left_side, right_side, (((1,), (1,)), ((), ())), preferre...  42.2 us
    dot_general x1, matrix products, attend_back(): jnp.einsum('bqkgd,bskd->bkgqs', grad_block, value_block, preferred_elemen...  38.7 us
  transfers between devices with their start and end apart: 24, of which 14 were waited for; matrix products, arithmetic and copies ran while one was open for 21% of the time, Pallas kernels for 0%

profile of v2, /device:TPU:0, one launch (start us, length us, event | category | flops | bytes accessed | tf_op | source)
XLA Modules:
  0.0 965.4 jit_solution(14312869714051228078)
XLA Ops:
  22.3 44.3 %all-gather.12.cloned.1.call-done = bf16[960,1152]{1,0:T(8,128)(2,1)} async-done(((bf16[120,1152]{1,0:T(8,128)(2,1)}), bf16[960,1152]{1,0:T(8,128)(2,1)}) %all-gather.12.cloned.1.call-update) | async-done | bytes 2211856 | tf_op jit(solution)/shard_map/all_gather | solution.py:215
  87.1 56.4 %all-gather.6.cloned.1.call-done = bf16[2,2048,256]{1,0,2:T(2,128)(2,1)} async-done(((bf16[2,256,256]{1,0,2:T(2,128)(2,1)}), bf16[2,2048,256]{1,0,2:T(2,128)(2,1)}) %all-gather.6.cloned.1.call-update) | async-done | bytes 2097168 | tf_op jit(solution)/shard_map/all_gather | solution.py:268
  146.8 21.3 %fusion.9 = (f32[2,2,7,256]{3,2,1,0:T(8,128)S(1)}, f32[2,2,2048,256,7]{3,2,4,1,0:T(8,128)}) fusion(pred[2,256,2048]{1,2,0:T(8,128)(4,1)S(1)} %compare_and_fusion, bf16[2,2048,2,64,1]{1,3,4,2,0:T(8,128)(2,1)S(1)} %bitcast.192, bf16[2,256,2,7,64]{1,0,4,3,2:T(2,128)(2,1)S(1)} %squeeze.71), kind=kOutput, calls=%fused_computation.14 | convolution fusion | flops 1923081216 | bytes 61763584 | tf_op jit(solution)/shard_map/while/body/eval_jaxpr/bqkgd,bskd->bkgqs/dot_general | solution.py:57
  168.2 19.1 %fusion.3 = f32[2,2,7,256]{3,2,1,0:T(8,128)S(1)} fusion(f32[2,2,7,256]{3,2,1,0:T(8,128)S(1)} %get-tuple-element.186, f32[2,2,2048,256,7]{3,2,4,1,0:T(8,128)} %get-tuple-element.187, pred[2,256,2048]{1,2,0:T(8,128)(4,1)S(1)} %compare_and_fusion), kind=kLoop, calls=%fused_computation.9 | loop fusion | flops 58713088 | bytes 59826176 | tf_op jit(solution)/shard_map/while/body/eval_jaxpr/reduce_sum | solution.py:68
  187.3 22.8 %fusion.52 = bf16[2,256,2,7,64]{1,4,3,2,0:T(8,128)(2,1)S(1)} fusion(bf16[2,2048,2,64,1]{1,3,4,2,0:T(8,128)(2,1)S(1)} %bitcast.197, f32[2,2,7,256]{3,2,1,0:T(8,128)S(1)} %fusion.3, f32[2,2,7,256]{3,2,1,0:T(8,128)S(1)} %get-tuple-element.186, f32[2,2,2048,256,7]{3,2,4,1,0:T(8,128)} %get-tuple-element.187, pred[2,256,2048]{1,2,0:T(8,128)(4,1)S(1)} %compare_and_fusion), kind=kOutput, calls=%fused_computation.100 | convolution fusion | flops 1952907264 | bytes 61792256 | tf_op jit(solution)/shard_map/while/body/eval_jaxpr/bkgqs,bskd->bqkgd/dot_general | solution.py:70
  212.3 30.0 %all-gather.8.cloned.1.call-done = bf16[896,3392]{1,0:T(8,128)(2,1)} async-done(((bf16[112,3392]{1,0:T(8,128)(2,1)}), bf16[896,3392]{1,0:T(8,128)(2,1)}) %all-gather.8.cloned.1.call-update) | async-done | bytes 6078480 | tf_op jit(solution)/shard_map/all_gather | solution.py:269
  248.2 20.1 %collective-permute-done = bf16[512,896]{1,0:T(8,128)(2,1)} collective-permute-done((bf16[512,896]{1,0:T(8,128)(2,1)}, bf16[512,896]{1,0:T(8,128)(2,1)}, u32[]{:S(2)}, u32[]{:S(2)}) %collective-permute-start) | collective-permute-done | bytes 917536 | tf_op jit(solution)/shard_map/ppermute | solution.py:105
  271.7 21.2 %collective-permute-done.4 = bf16[512,896]{1,0:T(8,128)(2,1)S(1)} collective-permute-done((bf16[512,896]{1,0:T(8,128)(2,1)S(1)}, bf16[512,896]{1,0:T(8,128)(2,1)S(1)}, u32[]{:S(2)}, u32[]{:S(2)}) %collective-permute-start.4) | collective-permute-done | bytes 917536 | tf_op jit(solution)/shard_map/ppermute | solution.py:105
  294.5 10.3 %fusion.24 = f32[2048,1216]{0,1:T(8,128)} fusion(bf16[896,3392]{1,0:T(8,128)(2,1)S(1)} %copy-done.37, bf16[1024,896]{1,0:T(8,128)(2,1)S(1)} %collective-permute-done.1, bf16[512,896]{1,0:T(8,128)(2,1)} %collective-permute-done, bf16[512,896]{1,0:T(8,128)(2,1)} %multiply_convert_fusion.3), kind=kOutput, calls=%fused_computation.53 | convolution fusion | flops 4473749504 | bytes 15925248 | tf_op jit(solution)/shard_map/dot_general | solution.py:288
  304.8 9.6 fusion.28
  314.5 18.4 %multiply_convert_fusion = (bf16[2048,1216]{0,1:T(8,128)(2,1)}, bf16[2048,1216]{0,1:T(8,128)(2,1)}, bf16[2048,1216]{0,1:T(8,128)(2,1)}) fusion(f32[2048,1216]{0,1:T(8,128)} %fusion.28, f32[2048,1216]{0,1:T(8,128)} %fusion.24, bf16[1216,896]{1,0:T(8,128)(2,1)} %all-gather.10.cloned.1.call-done, bf16[1024,896]{1,0:T(8,128)(2,1)} %collective-permute-done.5, ...), kind=kOutput, calls=%fused_computation.19 | convolution fusion | flops 4511105024 | bytes 40714240 | tf_op jit(solution)/shard_map/dot_general | solution.py:43
  332.8 8.6 convolution_convert_fusion.4
  341.7 7.6 fusion.26
  349.4 7.7 add_convert_fusion
  358.6 8.5 convolution_convert_fusion
  367.1 8.0 convolution_convert_fusion.1
  382.5 8.0 convolution_convert_fusion.3
  390.5 28.8 %collective-permute-done.7 = bf16[512,896]{1,0:T(8,128)(2,1)} collective-permute-done((bf16[512,896]{1,0:T(8,128)(2,1)}, bf16[512,896]{1,0:T(8,128)(2,1)}, u32[]{:S(2)}, u32[]{:S(2)}) %collective-permute-start.7) | collective-permute-done | bytes 917536 | tf_op jit(solution)/shard_map/ppermute | solution.py:105
  429.4 15.4 %fusion.13 = bf16[896,3392]{0,1:T(8,128)(2,1)} fusion(bf16[896,1216]{0,1:T(8,128)(2,1)S(1)} %copy-done.21, bf16[896,1216]{0,1:T(8,128)(2,1)S(1)} %copy-done.20, bf16[896,896]{0,1:T(8,128)(2,1)S(1)} %convolution_convert_fusion.5), kind=kLoop, calls=%fused_computation.25 | loop fusion | flops 30392320 | bytes 12042240 | tf_op jit(solution)/shard_map/concatenate | solution.py:308
  453.8 38.7 %fusion = (f32[2,2,7,256]{3,2,1,0:T(8,128)S(1)}, f32[2,2,2048,256,7]{3,2,4,1,0:T(8,128)}) fusion(f32[2,2,7,256]{3,2,1,0:T(8,128)S(1)} %copy-done.22, f32[2,2,2048,256,7]{3,2,4,1,0:T(8,128)} %get-tuple-element.187, pred[2,256,2048]{1,2,0:T(8,128)(4,1)S(1)} %copy-done.3, bf16[2,2048,2,64,1]{1,3,4,2,0:T(8,128)(2,1)} %bitcast.198, ...), kind=kOutput, calls=%fused_computation.2 | convolution fusion | flops 1952441344 | bytes 120512512 | tf_op jit(solution)/shard_map/while/body/eval_jaxpr/bqkgd,bskd->bkgqs/dot_general | solution.py:78
  492.4 22.1 %fusion.20 = bf16[2,2,64,2048]{3,2,1,0:T(8,128)(2,1)S(1)} fusion(bf16[2,256,2,7,64]{1,4,3,2,0:T(8,128)(2,1)S(1)} %copy-done.16, f32[2,2,7,256]{3,2,1,0:T(8,128)S(1)} %copy-done.22, f32[2,2,2048,256,7]{3,2,4,1,0:T(8,128)} %get-tuple-element.187, pred[2,256,2048]{1,2,0:T(8,128)(4,1)S(1)} %copy-done.3), kind=kOutput, calls=%fused_computation.45 | convolution fusion | flops 1938292736 | bytes 61763584 | tf_op jit(solution)/shard_map/while/body/eval_jaxpr/bkgqs,bqkgd->bskd/dot_general | solution.py:89
  514.5 46.5 %fusion.2 = bf16[2,2,7,256,2048]{3,4,2,1,0:T(8,128)(2,1)} fusion(f32[2,2,2048,256,7]{3,2,4,1,0:T(8,128)} %get-tuple-element.191, f32[2,2,7,256]{3,2,1,0:T(8,128)S(1)} %get-tuple-element.190, f32[2,2,7,256]{3,2,1,0:T(8,128)S(1)} %copy-done.22, f32[2,2,2048,256,7]{3,2,4,1,0:T(8,128)} %get-tuple-element.187, pred[2,256,2048]{1,2,0:T(8,128)(4,1)S(1)} %copy-done.3), kind=kLoop, calls=%fused_computation.4 | loop fusion | flops 88080384 | bytes 147906560 | tf_op jit(solution)/shard_map/while/body/eval_jaxpr/convert_element_type | solution.py:82
  561.1 14.5 %fusion.19 = bf16[2,2,64,2048]{3,2,1,0:T(8,128)(2,1)S(1)} fusion(bf16[2,2,7,256,2048]{3,4,2,1,0:T(8,128)(2,1)} %fusion.2, bf16[2,256,2,7,64]{1,0,4,3,2:T(2,128)(2,1)S(1)} %copy-done.10), kind=kOutput, calls=%fused_computation.44 | convolution fusion | flops 1880096768 | bytes 31326208 | tf_op jit(solution)/shard_map/while/body/eval_jaxpr/bkgqs,bqkgd->bskd/dot_general | solution.py:86
  579.7 12.3 %multiply_bitcast_fusion = f32[2,256,2,7,64]{1,4,3,2,0:T(8,128)S(1)} fusion(bf16[2,2048,2,64,1]{1,3,4,2,0:T(8,128)(2,1)S(1)} %bitcast.193, bf16[2,2,7,256,2048]{3,4,2,1,0:T(8,128)(2,1)} %fusion.2), kind=kOutput, calls=%fused_computation.87 | convolution fusion | flops 1879506944 | bytes 32243712 | tf_op jit(solution)/shard_map/while/body/eval_jaxpr/bkgqs,bskd->bqkgd/dot_general | solution.py:83
  598.2 47.2 %reduce-scatter.11.cloned.1.call-done = bf16[2,256,256]{2,1,0:T(8,128)(2,1)} async-done(((bf16[2,2048,256]{2,1,0:T(8,128)(2,1)}), bf16[2,256,256]{2,1,0:T(8,128)(2,1)}) %reduce-scatter.11.cloned.1.call-update) | async-done | bytes 262160 | tf_op jit(solution)/shard_map/reduce_scatter | solution.py:344
  647.3 5.0 fusion.45
  656.8 9.7 copy.142
  666.5 56.1 %reduce-scatter.17.cloned.1.call-done = bf16[152,896]{1,0:T(8,128)(2,1)} async-done(((bf16[1216,896]{1,0:T(8,128)(2,1)}), bf16[152,896]{1,0:T(8,128)(2,1)}) %reduce-scatter.17.cloned.1.call-update) | async-done | bytes 272400
  736.7 57.7 %reduce-scatter.15.cloned.1.call-done = bf16[1,120,1152]{2,1,0:T(8,128)(2,1)} async-done(((bf16[8,120,1152]{2,1,0:T(8,128)(2,1)}), bf16[1,120,1152]{2,1,0:T(8,128)(2,1)}) %reduce-scatter.15.cloned.1.call-update) | async-done | bytes 276496
  797.8 116.8 %reduce-scatter.13.cloned.1.call-done = bf16[112,3392]{1,0:T(8,128)(2,1)} async-done(((bf16[896,3392]{1,0:T(8,128)(2,1)}), bf16[112,3392]{1,0:T(8,128)(2,1)}) %reduce-scatter.13.cloned.1.call-update) | async-done | bytes 759824
  921.4 9.7 %collective-permute-done.12 = bf16[1,112,2496]{2,1,0:T(8,128)(2,1)S(1)} collective-permute-done((bf16[1,112,2496]{2,1,0:T(8,128)(2,1)S(1)}, bf16[1,112,2496]{2,1,0:T(8,128)(2,1)S(1)}, u32[]{:S(2)}, u32[]{:S(2)}) %collective-permute-start.12) | collective-permute-done | bytes 559136 | tf_op jit(solution)/shard_map/ppermute | solution.py:105
  938.8 5.8 collective-permute-done.11
  (278 shorter events, 134.0 us)
Async XLA Ops:
  7.2 59.4 %all-gather.12.cloned.1.call-start = ((), (), s32[]{:S(2)}) async-start(), calls=%async_computation.8 | async-start | bytes 2488320 | tf_op jit(solution)/shard_map/all_gather | solution.py:215
  13.2 130.2 %all-gather.6.cloned.1.call-start = ((), (), s32[]{:S(2)}) async-start(), calls=%async_computation.4 | async-start | bytes 2359296 | tf_op jit(solution)/shard_map/all_gather | solution.py:268
  82.0 160.2 %all-gather.8.cloned.1.call-start = ((), (), s32[]{:S(2)}) async-start(), calls=%async_computation.5 | async-start | bytes 6967296 | tf_op jit(solution)/shard_map/all_gather | solution.py:269
  82.7 64.1 %copy-start.9 = (bf16[2,256,2,7,64]{1,0,4,3,2:T(2,128)(2,1)}, bf16[2,256,2,7,64]{1,0,4,3,2:T(2,128)(2,1)S(1)}, u32[]{:S(2)}) copy-start(bf16[2,256,2,7,64]{1,0,4,3,2:T(2,128)(2,1)S(1)} %squeeze.71) | copy-start | bytes 2752516
  86.5 100.9 %copy-start.2 = (pred[2,256,2048]{1,2,0:T(8,128)(4,1)}, pred[2,256,2048]{1,2,0:T(8,128)(4,1)S(1)}, u32[]{:S(2)}) copy-start(pred[2,256,2048]{1,2,0:T(8,128)(4,1)S(1)} %compare_and_fusion) | copy-start | bytes 3145732
  86.5 228.0 %all-gather.10.cloned.1.call-start = ((), (), s32[]{:S(2)}) async-start(), calls=%async_computation.6 | async-start | bytes 2451456 | tf_op jit(solution)/shard_map/all_gather | solution.py:270
  146.8 40.5 %copy-start.17 = (bf16[2,2048,128]{1,2,0:T(8,128)(2,1)}, bf16[2,2048,128]{1,2,0:T(8,128)(2,1)S(1)}, u32[]{:S(2)}) copy-start(bf16[2,2048,128]{1,2,0:T(8,128)(2,1)S(1)} %copy.106) | copy-start | bytes 3145732
  246.5 21.8 %collective-permute-start = (bf16[512,896]{1,0:T(8,128)(2,1)}, bf16[512,896]{1,0:T(8,128)(2,1)}, u32[]{:S(2)}, u32[]{:S(2)}) collective-permute-start(bf16[512,896]{1,0:T(8,128)(2,1)} %multiply_convert_fusion.3), channel_id=1, source_target_pairs={{0,16},{8,24},{16,0},{24,8},{1,17},{9,25},{17,1},{25,9},{2,18},{10... | collective-permute-start | bytes 2752520 | tf_op jit(solution)/shard_map/ppermute | solution.py:105
  248.0 397.4 %reduce-scatter.11.cloned.1.call-start = ((), (), s32[]{:S(2)}) async-start(), calls=%async_computation.7 | async-start | bytes 2359296 | tf_op jit(solution)/shard_map/reduce_scatter | solution.py:344
  270.1 24.4 %collective-permute-start.1 = (bf16[1024,896]{1,0:T(8,128)(2,1)S(1)}, bf16[1024,896]{1,0:T(8,128)(2,1)S(1)}, u32[]{:S(2)}, u32[]{:S(2)}) collective-permute-start(bf16[1024,896]{1,0:T(8,128)(2,1)S(1)} %pad_maximum_fusion.5), channel_id=1, source_target_pairs={{0,8},{8,0},{16,24},{24,16},{1,9},{9,1},{17,25},{25,17},{2,10},{10... | collective-permute-start | bytes 5505032 | tf_op jit(solution)/shard_map/ppermute | solution.py:105
  270.2 22.8 %collective-permute-start.4 = (bf16[512,896]{1,0:T(8,128)(2,1)S(1)}, bf16[512,896]{1,0:T(8,128)(2,1)S(1)}, u32[]{:S(2)}, u32[]{:S(2)}) collective-permute-start(bf16[512,896]{1,0:T(8,128)(2,1)S(1)} %bitcast.200), channel_id=1, source_target_pairs={{0,16},{8,24},{16,0},{24,8},{1,17},{9,25},{17,1},{25,9},{2,18},{10... | collective-permute-start | bytes 2752520 | tf_op jit(solution)/shard_map/ppermute | solution.py:105
  293.1 21.4 %collective-permute-start.5 = (bf16[1024,896]{1,0:T(8,128)(2,1)S(1)}, bf16[1024,896]{1,0:T(8,128)(2,1)}, u32[]{:S(2)}, u32[]{:S(2)}) collective-permute-start(bf16[1024,896]{1,0:T(8,128)(2,1)S(1)} %pad_maximum_fusion.6), channel_id=1, source_target_pairs={{0,8},{8,0},{16,24},{24,16},{1,9},{9,1},{17,25},{25,17},{2,10},{10... | collective-permute-start | bytes 5505032 | tf_op jit(solution)/shard_map/ppermute | solution.py:105
  341.6 33.4 %collective-permute-start.2 = (bf16[1024,896]{1,0:T(8,128)(2,1)S(1)}, bf16[1024,896]{1,0:T(8,128)(2,1)S(1)}, u32[]{:S(2)}, u32[]{:S(2)}) collective-permute-start(bf16[1024,896]{1,0:T(8,128)(2,1)S(1)} %slice.236), channel_id=1, source_target_pairs={{0,8},{8,0},{16,24},{24,16},{1,9},{9,1},{17,25},{25,17},{2,10},{10... | collective-permute-start | bytes 5505032 | tf_op jit(solution)/shard_map/ppermute | solution.py:105
  357.3 20.7 %collective-permute-start.6 = (bf16[1024,896]{1,0:T(8,128)(2,1)S(1)}, bf16[1024,896]{1,0:T(8,128)(2,1)S(1)}, u32[]{:S(2)}, u32[]{:S(2)}) collective-permute-start(bf16[1024,896]{1,0:T(8,128)(2,1)S(1)} %slice.240), channel_id=1, source_target_pairs={{0,8},{8,0},{16,24},{24,16},{1,9},{9,1},{17,25},{25,17},{2,10},{10... | collective-permute-start | bytes 5505032 | tf_op jit(solution)/shard_map/ppermute | solution.py:105
  376.5 46.0 %collective-permute-start.3 = (bf16[512,896]{1,0:T(8,128)(2,1)}, bf16[512,896]{1,0:T(8,128)(2,1)}, u32[]{:S(2)}, u32[]{:S(2)}) collective-permute-start(bf16[512,896]{1,0:T(8,128)(2,1)} %slice.309), channel_id=1, source_target_pairs={{0,16},{8,24},{16,0},{24,8},{1,17},{9,25},{17,1},{25,9},{2,18},{10... | collective-permute-start | bytes 2752520 | tf_op jit(solution)/shard_map/ppermute | solution.py:105
  381.2 38.2 %collective-permute-start.7 = (bf16[512,896]{1,0:T(8,128)(2,1)}, bf16[512,896]{1,0:T(8,128)(2,1)}, u32[]{:S(2)}, u32[]{:S(2)}) collective-permute-start(bf16[512,896]{1,0:T(8,128)(2,1)} %slice.308), channel_id=1, source_target_pairs={{0,16},{8,24},{16,0},{24,8},{1,17},{9,25},{17,1},{25,9},{2,18},{10... | collective-permute-start | bytes 2752520 | tf_op jit(solution)/shard_map/ppermute | solution.py:105
  514.5 46.6 %copy-start.10 = (bf16[2,256,2,7,64]{1,0,4,3,2:T(2,128)(2,1)S(1)}, bf16[2,256,2,7,64]{1,0,4,3,2:T(2,128)(2,1)}, u32[]{:S(2)}) copy-start(bf16[2,256,2,7,64]{1,0,4,3,2:T(2,128)(2,1)} %copy-done.9) | copy-start | bytes 2752516
  578.5 144.0 %reduce-scatter.17.cloned.1.call-start = ((), (), s32[]{:S(2)}) async-start(), calls=%async_computation.11 | async-start | bytes 2451456
  579.1 215.3 %reduce-scatter.15.cloned.1.call-start = ((), (), s32[]{:S(2)}) async-start(), calls=%async_computation.10 | async-start | bytes 2488320
  598.1 49.2 %copy-start.13 = (bf16[2,256,896]{2,1,0:T(8,128)(2,1)S(1)}, bf16[2,256,896]{2,1,0:T(8,128)(2,1)}, u32[]{:S(2)}) copy-start(bf16[2,256,896]{2,1,0:T(8,128)(2,1)} %param.17) | copy-start | bytes 2752516
  598.1 49.1 %copy-start.32 = (f32[896]{0:T(1024)S(1)}, f32[896]{0:T(1024)}, u32[]{:S(2)}) copy-start(f32[896]{0:T(1024)} %copy-done.31) | copy-start | bytes 10756
  656.7 257.9 %reduce-scatter.13.cloned.1.call-start = ((), (), s32[]{:S(2)}) async-start(), calls=%async_computation.9 | async-start | bytes 6967296
  666.4 57.6 %copy-start.35 = (s32[4]{0:T(128)S(1)}, s32[4]{0:T(128)}, u32[]{:S(2)}) copy-start(s32[4]{0:T(128)} %constant.127.clone) | copy-start | bytes 52
  666.4 67.1 %copy-start.15 = (f32[512,896]{1,0:T(8,128)S(1)}, f32[512,896]{1,0:T(8,128)}, u32[]{:S(2)}) copy-start(f32[512,896]{1,0:T(8,128)} %copy-done.14) | copy-start | bytes 5505028
  722.5 9.8 %collective-permute-start.14 = (bf16[1,152,896]{2,1,0:T(8,128)(2,1)}, bf16[1,152,896]{2,1,0:T(8,128)(2,1)S(1)}, u32[]{:S(2)}, u32[]{:S(2)}) collective-permute-start(bf16[1,152,896]{2,1,0:T(8,128)(2,1)} %bitcast.217), channel_id=1, source_target_pairs={{0,16},{8,24},{16,0},{24,8},{1,17},{9,25},{17,1},{25,9},{2,18},{10... | collective-permute-start | bytes 817160 | tf_op jit(solution)/shard_map/ppermute | solution.py:105
  733.5 3.1 collective-permute-start.15
  794.4 1.8 collective-permute-start.8
  796.3 123.2 %collective-permute-start.9 = (bf16[120,1152]{1,0:T(8,128)(2,1)S(1)}, bf16[120,1152]{1,0:T(8,128)(2,1)}, u32[]{:S(2)}, u32[]{:S(2)}) collective-permute-start(bf16[120,1152]{1,0:T(8,128)(2,1)S(1)} %add_convert_fusion.3), channel_id=1, source_target_pairs={{0,16},{8,24},{16,0},{24,8},{1,17},{9,25},{17,1},{25,9},{2,18},{10... | collective-permute-start | bytes 829448 | tf_op jit(solution)/shard_map/ppermute | solution.py:105
  916.3 14.8 %collective-permute-start.12 = (bf16[1,112,2496]{2,1,0:T(8,128)(2,1)S(1)}, bf16[1,112,2496]{2,1,0:T(8,128)(2,1)S(1)}, u32[]{:S(2)}, u32[]{:S(2)}) collective-permute-start(bf16[1,112,2496]{2,1,0:T(8,128)(2,1)S(1)} %copy.124), channel_id=1, source_target_pairs={{0,16},{8,24},{16,0},{24,8},{1,17},{9,25},{17,1},{25,9},{2,18},{10... | collective-permute-start | bytes 1677320 | tf_op jit(solution)/shard_map/ppermute | solution.py:105
  933.2 12.4 %collective-permute-start.13 = (bf16[2,112,2496]{2,1,0:T(8,128)(2,1)}, bf16[2,112,2496]{2,1,0:T(8,128)(2,1)}, u32[]{:S(2)}, u32[]{:S(2)}) collective-permute-start(bf16[2,112,2496]{2,1,0:T(8,128)(2,1)} %copy.126), channel_id=1, source_target_pairs={{0,8},{8,0},{16,24},{24,16},{1,9},{9,1},{17,25},{25,17},{2,10},{10... | collective-permute-start | bytes 3354632 | tf_op jit(solution)/shard_map/ppermute | solution.py:105
  934.9 1.7 collective-permute-start.10
  936.6 7.9 collective-permute-start.11
  (40 other events, 339.8 us)
Sparse Core Ops, SparseCore 0:
  13.3 53.2 all-gather.11
  82.1 61.2 all-gather.5
  146.2 96.0 all-gather.7
  248.1 47.5 all-gather.9
  578.6 66.7 reduce-scatter.10
  649.3 73.1 reduce-scatter.16
  726.5 67.8 reduce-scatter.14
  798.1 116.4 reduce-scatter.12

commit v3 on v2

--- a/solution.py
+++ b/solution.py
@@ -341,6 +341,9 @@
         ],
         axis=2,
     )
+    grad_key_values, later_owned, down_owned = lax.optimization_barrier(
+        (grad_key_values, later_owned, down_owned)
+    )
     grad_key_values = lax.psum_scatter(
         grad_key_values, "shard", scatter_dimension=1, tiled=True
     ).reshape(row_count, 2 * key_width)

time: 972 us -> 838 us (0.86)
  waiting for transfers between devices: 497 us -> 351 us
    unnamed x11 -> x10, waiting for transfers between devices: 231 us -> 17.9 us
    optimization_barrier x0 -> x1, waiting for transfers between devices: none -> 57.5 us  [on_device(): lax.optimization_barrier((grad_key_values, later_owned, down_owned))]
    unnamed x112 -> x114, local copies, waits for them, and re-layouts: 30.8 us -> 31.7 us
  transfers between devices with their start and end apart: 24 -> 24, of which waited for: 14 -> 11; matrix products, arithmetic and copies ran while one was open for 21% -> 41% of each run, Pallas kernels for 0% -> 0%
where the time goes in v3:
time: 838 us; the launch traced here: 832 us
  waiting for transfers between devices  351 us (42%)
  matrix products  236 us (28%)
  other arithmetic  125 us (15%)
  local copies, waits for them, and re-layouts  83.7 us (10%)
  between operations  23.4 us (3%)
  starting transfers between devices  12.1 us (1%)
    ppermute x16, waiting for transfers between devices, partner_swap(): return lax.ppermute(values, 'rep', [(i, i ^ bit) for i in range(reps)])  92.1 us
    optimization_barrier x1, waiting for transfers between devices, on_device(): lax.optimization_barrier((grad_key_values, later_owned, down_owned))  57.5 us
    all_gather x1, waiting for transfers between devices, on_device(): key_values = lax.all_gather(key_values, 'shard', axis=1, tiled=True)  56.4 us
    reduce_scatter x1, waiting for transfers between devices, on_device(): lax.psum_scatter(grad_key_values, 'shard', scatter_dimension=1, tiled=True)  53.3 us
    convert_element_type x1, other arithmetic, attend_back(): grad_scores = (probs_full * (grad_probs - row_delta)).astype(jnp.bfloat16)  48.3 us
    all_gather x1, waiting for transfers between devices, on_device(): lax.all_gather(jnp.concatenate([qkv_part, small], axis=0), 'shard', axis=...  44.3 us
    dot_general x5, matrix products, times_transposed(): lax.dot_general(left_side, right_side, (((1,), (1,)), ((), ())), preferre...  41.6 us
    dot_general x1, matrix products, attend_back(): jnp.einsum('bqkgd,bskd->bkgqs', grad_block, value_block, preferred_elemen...  38.6 us
  transfers between devices with their start and end apart: 24, of which 11 were waited for; matrix products, arithmetic and copies ran while one was open for 41% of the time, Pallas kernels for 0%

profile of v3, /device:TPU:0, one launch (start us, length us, event | category | flops | bytes accessed | tf_op | source)
XLA Modules:
  0.0 831.8 jit_solution(1483413897812998237)
XLA Ops:
  8.0 3.4 concatenate.89
  22.3 44.3 %all-gather.12.cloned.1.call-done = bf16[960,1152]{1,0:T(8,128)(2,1)} async-done(((bf16[120,1152]{1,0:T(8,128)(2,1)}), bf16[960,1152]{1,0:T(8,128)(2,1)}) %all-gather.12.cloned.1.call-update) | async-done | bytes 2211856 | tf_op jit(solution)/shard_map/all_gather | solution.py:215
  87.0 56.4 %all-gather.6.cloned.1.call-done = bf16[2,2048,256]{1,0,2:T(2,128)(2,1)} async-done(((bf16[2,256,256]{1,0,2:T(2,128)(2,1)}), bf16[2,2048,256]{1,0,2:T(2,128)(2,1)}) %all-gather.6.cloned.1.call-update) | async-done | bytes 2097168 | tf_op jit(solution)/shard_map/all_gather | solution.py:268
  146.8 21.3 %fusion.9 = (f32[2,2,7,256]{3,2,1,0:T(8,128)S(1)}, f32[2,2,2048,256,7]{3,2,4,1,0:T(8,128)}) fusion(pred[2,256,2048]{1,2,0:T(8,128)(4,1)S(1)} %compare_and_fusion, bf16[2,2048,2,64,1]{1,3,4,2,0:T(8,128)(2,1)S(1)} %bitcast.190, bf16[2,256,2,7,64]{1,0,4,3,2:T(2,128)(2,1)S(1)} %squeeze.71), kind=kOutput, calls=%fused_computation.14 | convolution fusion | flops 1923081216 | bytes 61763584 | tf_op jit(solution)/shard_map/while/body/eval_jaxpr/bqkgd,bskd->bkgqs/dot_general | solution.py:57
  168.2 19.1 %fusion.3 = f32[2,2,7,256]{3,2,1,0:T(8,128)S(1)} fusion(f32[2,2,7,256]{3,2,1,0:T(8,128)S(1)} %get-tuple-element.192, f32[2,2,2048,256,7]{3,2,4,1,0:T(8,128)} %get-tuple-element.193, pred[2,256,2048]{1,2,0:T(8,128)(4,1)S(1)} %compare_and_fusion), kind=kLoop, calls=%fused_computation.9 | loop fusion | flops 58713088 | bytes 59826176 | tf_op jit(solution)/shard_map/while/body/eval_jaxpr/reduce_sum | solution.py:68
  187.3 22.8 %fusion.52 = bf16[2,256,2,7,64]{1,4,3,2,0:T(8,128)(2,1)S(1)} fusion(bf16[2,2048,2,64,1]{1,3,4,2,0:T(8,128)(2,1)S(1)} %bitcast.195, f32[2,2,7,256]{3,2,1,0:T(8,128)S(1)} %fusion.3, f32[2,2,7,256]{3,2,1,0:T(8,128)S(1)} %get-tuple-element.192, f32[2,2,2048,256,7]{3,2,4,1,0:T(8,128)} %get-tuple-element.193, pred[2,256,2048]{1,2,0:T(8,128)(4,1)S(1)} %compare_and_fusion), kind=kOutput, calls=%fused_computation.100 | convolution fusion | flops 1952907264 | bytes 61792256 | tf_op jit(solution)/shard_map/while/body/eval_jaxpr/bkgqs,bskd->bqkgd/dot_general | solution.py:70
  212.3 30.0 %all-gather.8.cloned.1.call-done = bf16[896,3392]{1,0:T(8,128)(2,1)} async-done(((bf16[112,3392]{1,0:T(8,128)(2,1)}), bf16[896,3392]{1,0:T(8,128)(2,1)}) %all-gather.8.cloned.1.call-update) | async-done | bytes 6078480 | tf_op jit(solution)/shard_map/all_gather | solution.py:269
  248.2 20.1 %collective-permute-done = bf16[512,896]{1,0:T(8,128)(2,1)} collective-permute-done((bf16[512,896]{1,0:T(8,128)(2,1)}, bf16[512,896]{1,0:T(8,128)(2,1)}, u32[]{:S(2)}, u32[]{:S(2)}) %collective-permute-start) | collective-permute-done | bytes 917536 | tf_op jit(solution)/shard_map/ppermute | solution.py:105
  271.7 21.2 %collective-permute-done.4 = bf16[512,896]{1,0:T(8,128)(2,1)S(1)} collective-permute-done((bf16[512,896]{1,0:T(8,128)(2,1)S(1)}, bf16[512,896]{1,0:T(8,128)(2,1)S(1)}, u32[]{:S(2)}, u32[]{:S(2)}) %collective-permute-start.4) | collective-permute-done | bytes 917536 | tf_op jit(solution)/shard_map/ppermute | solution.py:105
  293.9 10.3 %fusion.24 = f32[2048,1216]{0,1:T(8,128)} fusion(bf16[896,3392]{1,0:T(8,128)(2,1)S(1)} %copy-done.41, bf16[1024,896]{1,0:T(8,128)(2,1)S(1)} %collective-permute-done.1, bf16[512,896]{1,0:T(8,128)(2,1)} %collective-permute-done, bf16[512,896]{1,0:T(8,128)(2,1)} %multiply_convert_fusion.3), kind=kOutput, calls=%fused_computation.53 | convolution fusion | flops 4473749504 | bytes 15925248 | tf_op jit(solution)/shard_map/dot_general | solution.py:288
  304.2 9.6 %fusion.28 = f32[2048,1216]{0,1:T(8,128)} fusion(bf16[896,3392]{1,0:T(8,128)(2,1)S(1)} %copy-done.41, bf16[1024,896]{1,0:T(8,128)(2,1)S(1)} %collective-permute-done.1, bf16[512,896]{1,0:T(8,128)(2,1)} %collective-permute-done, bf16[512,896]{1,0:T(8,128)(2,1)} %multiply_convert_fusion.3), kind=kOutput, calls=%fused_computation.57 | convolution fusion | flops 4473749504 | bytes 15925248 | tf_op jit(solution)/shard_map/dot_general | solution.py:287
  313.8 18.4 %multiply_convert_fusion = (bf16[2048,1216]{0,1:T(8,128)(2,1)}, bf16[2048,1216]{0,1:T(8,128)(2,1)}, bf16[2048,1216]{0,1:T(8,128)(2,1)}) fusion(f32[2048,1216]{0,1:T(8,128)} %fusion.28, f32[2048,1216]{0,1:T(8,128)} %fusion.24, bf16[1216,896]{1,0:T(8,128)(2,1)} %all-gather.10.cloned.1.call-done, bf16[1024,896]{1,0:T(8,128)(2,1)} %collective-permute-done.5, ...), kind=kOutput, calls=%fused_computation.19 | convolution fusion | flops 4511105024 | bytes 40714240 | tf_op jit(solution)/shard_map/dot_general | solution.py:43
  332.2 8.6 %convolution_convert_fusion.4 = bf16[2048,896]{1,0:T(8,128)(2,1)S(1)} fusion(bf16[2048,1216]{0,1:T(8,128)(2,1)} %get-tuple-element.145, bf16[1216,896]{1,0:T(8,128)(2,1)} %all-gather.10.cloned.1.call-done), kind=kOutput, calls=%fused_computation.37 | convolution fusion | flops 4464574464 | bytes 10829824 | tf_op jit(solution)/shard_map/dot_general | solution.py:327
  344.1 7.9 fusion.26
  352.1 7.8 add_convert_fusion
  363.1 8.4 %convolution_convert_fusion.3 = bf16[1216,896]{1,0:T(8,128)(2,1)} fusion(bf16[2048,1216]{0,1:T(8,128)(2,1)S(1)} %bitcast.246, bf16[1024,896]{1,0:T(8,128)(2,1)} %collective-permute-done.5, bf16[512,896]{1,0:T(8,128)(2,1)S(1)} %copy-done.26, bf16[512,896]{1,0:T(8,128)(2,1)S(1)} %bitcast.201), kind=kOutput, calls=%fused_computation.36 | convolution fusion | flops 4474839040 | bytes 10829824 | tf_op jit(solution)/shard_map/dot_general | solution.py:37
  371.6 8.4 %convolution_convert_fusion = bf16[896,1216]{0,1:T(8,128)(2,1)S(1)} fusion(bf16[2048,1216]{0,1:T(8,128)(2,1)} %get-tuple-element.143, bf16[1024,896]{1,0:T(8,128)(2,1)} %copy-done.42, bf16[512,896]{1,0:T(8,128)(2,1)} %collective-permute-done, bf16[512,896]{1,0:T(8,128)(2,1)} %multiply_convert_fusion.3), kind=kOutput, calls=%fused_computation.33 | convolution fusion | flops 4474839040 | bytes 10829824 | tf_op jit(solution)/shard_map/dot_general | solution.py:37
  386.3 7.7 convolution_convert_fusion.1
  394.0 30.6 %collective-permute-done.7 = bf16[512,896]{1,0:T(8,128)(2,1)S(1)} collective-permute-done((bf16[512,896]{1,0:T(8,128)(2,1)S(1)}, bf16[512,896]{1,0:T(8,128)(2,1)S(1)}, u32[]{:S(2)}, u32[]{:S(2)}) %collective-permute-start.7) | collective-permute-done | bytes 917536 | tf_op jit(solution)/shard_map/ppermute | solution.py:105
  428.8 15.4 %fusion.13 = bf16[896,3392]{0,1:T(8,128)(2,1)} fusion(bf16[896,1216]{0,1:T(8,128)(2,1)S(1)} %convolution_convert_fusion.1, bf16[896,1216]{0,1:T(8,128)(2,1)S(1)} %convolution_convert_fusion, bf16[896,896]{0,1:T(8,128)(2,1)S(1)} %convolution_convert_fusion.5), kind=kLoop, calls=%fused_computation.25 | loop fusion | flops 30392320 | bytes 12042240 | tf_op jit(solution)/shard_map/concatenate | solution.py:308
  446.8 9.2 %copy.142 = bf16[896,3392]{1,0:T(8,128)(2,1)} copy(bf16[896,3392]{0,1:T(8,128)(2,1)} %fusion.13) | data formatting | bytes 12156928
  462.2 38.6 %fusion = (f32[2,2,7,256]{3,2,1,0:T(8,128)S(1)}, f32[2,2,2048,256,7]{3,2,4,1,0:T(8,128)}) fusion(f32[2,2,7,256]{3,2,1,0:T(8,128)S(1)} %log_add_fusion, f32[2,2,2048,256,7]{3,2,4,1,0:T(8,128)} %get-tuple-element.193, pred[2,256,2048]{1,2,0:T(8,128)(4,1)S(1)} %copy-done.3, bf16[2,2048,2,64,1]{1,3,4,2,0:T(8,128)(2,1)S(1)} %bitcast.196, ...), kind=kOutput, calls=%fused_computation.2 | convolution fusion | flops 1952441344 | bytes 120512512 | tf_op jit(solution)/shard_map/while/body/eval_jaxpr/bqkgd,bskd->bkgqs/dot_general | solution.py:78
  500.7 48.3 %fusion.2 = bf16[2,2,7,256,2048]{3,4,2,1,0:T(8,128)(2,1)} fusion(f32[2,2,2048,256,7]{3,2,4,1,0:T(8,128)} %get-tuple-element.197, f32[2,2,7,256]{3,2,1,0:T(8,128)S(1)} %get-tuple-element.196, f32[2,2,7,256]{3,2,1,0:T(8,128)S(1)} %log_add_fusion, f32[2,2,2048,256,7]{3,2,4,1,0:T(8,128)} %get-tuple-element.193, pred[2,256,2048]{1,2,0:T(8,128)(4,1)S(1)} %copy-done.3), kind=kLoop, calls=%fused_computation.4 | loop fusion | flops 88080384 | bytes 147906560 | tf_op jit(solution)/shard_map/while/body/eval_jaxpr/convert_element_type | solution.py:82
  549.0 23.1 %fusion.20 = bf16[2,2,64,2048]{3,2,1,0:T(8,128)(2,1)} fusion(bf16[2,256,2,7,64]{1,4,3,2,0:T(8,128)(2,1)S(1)} %copy-done.13, f32[2,2,7,256]{3,2,1,0:T(8,128)S(1)} %log_add_fusion, f32[2,2,2048,256,7]{3,2,4,1,0:T(8,128)} %get-tuple-element.193, pred[2,256,2048]{1,2,0:T(8,128)(4,1)S(1)} %copy-done.3), kind=kOutput, calls=%fused_computation.45 | convolution fusion | flops 1938292736 | bytes 61763584 | tf_op jit(solution)/shard_map/while/body/eval_jaxpr/bkgqs,bqkgd->bskd/dot_general | solution.py:89
  573.8 14.5 %fusion.19 = bf16[2,2,64,2048]{3,2,1,0:T(8,128)(2,1)S(1)} fusion(bf16[2,2,7,256,2048]{3,4,2,1,0:T(8,128)(2,1)} %fusion.2, bf16[2,256,2,7,64]{1,0,4,3,2:T(2,128)(2,1)S(1)} %copy-done.8), kind=kOutput, calls=%fused_computation.44 | convolution fusion | flops 1880096768 | bytes 31326208 | tf_op jit(solution)/shard_map/while/body/eval_jaxpr/bkgqs,bqkgd->bskd/dot_general | solution.py:86
  592.9 57.5 %reduce-scatter.15.cloned.1.call-done = bf16[152,896]{1,0:T(8,128)(2,1)} async-done(((bf16[1216,896]{1,0:T(8,128)(2,1)}), bf16[152,896]{1,0:T(8,128)(2,1)}) %reduce-scatter.15.cloned.1.call-update) | async-done | bytes 272400 | tf_op jit(solution)/shard_map/optimization_barrier | solution.py:344
  650.6 12.2 %multiply_bitcast_fusion = f32[2,256,2,7,64]{1,4,3,2,0:T(8,128)S(1)} fusion(bf16[2,2048,2,64,1]{1,3,4,2,0:T(8,128)(2,1)S(1)} %bitcast.191, bf16[2,2,7,256,2048]{3,4,2,1,0:T(8,128)(2,1)} %fusion.2), kind=kOutput, calls=%fused_computation.87 | convolution fusion | flops 1879506944 | bytes 32243712 | tf_op jit(solution)/shard_map/while/body/eval_jaxpr/bkgqs,bskd->bqkgd/dot_general | solution.py:83
  668.7 53.3 %reduce-scatter.11.cloned.1.call-done = bf16[2,256,256]{2,1,0:T(8,128)(2,1)} async-done(((bf16[2,2048,256]{2,1,0:T(8,128)(2,1)}), bf16[2,256,256]{2,1,0:T(8,128)(2,1)}) %reduce-scatter.11.cloned.1.call-update) | async-done | bytes 262160 | tf_op jit(solution)/shard_map/reduce_scatter | solution.py:347
  723.9 4.8 fusion.45
  737.7 17.2 %collective-permute-done.14 = bf16[1,152,896]{2,1,0:T(8,128)(2,1)S(1)} collective-permute-done((bf16[1,152,896]{2,1,0:T(8,128)(2,1)S(1)}, bf16[1,152,896]{2,1,0:T(8,128)(2,1)S(1)}, u32[]{:S(2)}, u32[]{:S(2)}) %collective-permute-start.14) | collective-permute-done | bytes 272416 | tf_op jit(solution)/shard_map/ppermute | solution.py:105
  782.0 17.7 %reduce-scatter.17.cloned.1.call-done = bf16[1,120,1152]{2,1,0:T(8,128)(2,1)} async-done(((bf16[8,120,1152]{2,1,0:T(8,128)(2,1)}), bf16[1,120,1152]{2,1,0:T(8,128)(2,1)}) %reduce-scatter.17.cloned.1.call-update) | async-done | bytes 276496
  815.2 3.6 fusion.39
  (279 shorter events, 136.4 us)
Async XLA Ops:
  7.2 59.4 %all-gather.12.cloned.1.call-start = ((), (), s32[]{:S(2)}) async-start(), calls=%async_computation.8 | async-start | bytes 2488320 | tf_op jit(solution)/shard_map/all_gather | solution.py:215
  13.2 130.1 %all-gather.6.cloned.1.call-start = ((), (), s32[]{:S(2)}) async-start(), calls=%async_computation.4 | async-start | bytes 2359296 | tf_op jit(solution)/shard_map/all_gather | solution.py:268
  82.0 160.3 %all-gather.8.cloned.1.call-start = ((), (), s32[]{:S(2)}) async-start(), calls=%async_computation.5 | async-start | bytes 6967296 | tf_op jit(solution)/shard_map/all_gather | solution.py:269
  82.7 64.0 %copy-start.7 = (bf16[2,256,2,7,64]{1,0,4,3,2:T(2,128)(2,1)}, bf16[2,256,2,7,64]{1,0,4,3,2:T(2,128)(2,1)S(1)}, u32[]{:S(2)}) copy-start(bf16[2,256,2,7,64]{1,0,4,3,2:T(2,128)(2,1)S(1)} %squeeze.71) | copy-start | bytes 2752516
  86.4 100.9 %copy-start.2 = (pred[2,256,2048]{1,2,0:T(8,128)(4,1)}, pred[2,256,2048]{1,2,0:T(8,128)(4,1)S(1)}, u32[]{:S(2)}) copy-start(pred[2,256,2048]{1,2,0:T(8,128)(4,1)S(1)} %compare_and_fusion) | copy-start | bytes 3145732
  86.4 227.4 %all-gather.10.cloned.1.call-start = ((), (), s32[]{:S(2)}) async-start(), calls=%async_computation.6 | async-start | bytes 2451456 | tf_op jit(solution)/shard_map/all_gather | solution.py:270
  146.8 40.5 %copy-start.15 = (bf16[2,2048,128]{1,2,0:T(8,128)(2,1)}, bf16[2,2048,128]{1,2,0:T(8,128)(2,1)S(1)}, u32[]{:S(2)}) copy-start(bf16[2,2048,128]{1,2,0:T(8,128)(2,1)S(1)} %copy.106) | copy-start | bytes 3145732
  246.5 21.9 %collective-permute-start = (bf16[512,896]{1,0:T(8,128)(2,1)}, bf16[512,896]{1,0:T(8,128)(2,1)}, u32[]{:S(2)}, u32[]{:S(2)}) collective-permute-start(bf16[512,896]{1,0:T(8,128)(2,1)} %multiply_convert_fusion.3), channel_id=1, source_target_pairs={{0,16},{8,24},{16,0},{24,8},{1,17},{9,25},{17,1},{25,9},{2,18},{10... | collective-permute-start | bytes 2752520 | tf_op jit(solution)/shard_map/ppermute | solution.py:105
  248.0 342.6 %reduce-scatter.13.cloned.1.call-start = ((), (), s32[]{:S(2)}) async-start(), calls=%async_computation.9 | async-start | bytes 6967296
  270.1 23.8 %collective-permute-start.1 = (bf16[1024,896]{1,0:T(8,128)(2,1)S(1)}, bf16[1024,896]{1,0:T(8,128)(2,1)S(1)}, u32[]{:S(2)}, u32[]{:S(2)}) collective-permute-start(bf16[1024,896]{1,0:T(8,128)(2,1)S(1)} %pad_maximum_fusion.5), channel_id=1, source_target_pairs={{0,8},{8,0},{16,24},{24,16},{1,9},{9,1},{17,25},{25,17},{2,10},{10... | collective-permute-start | bytes 5505032 | tf_op jit(solution)/shard_map/ppermute | solution.py:105
  270.2 22.8 %collective-permute-start.4 = (bf16[512,896]{1,0:T(8,128)(2,1)S(1)}, bf16[512,896]{1,0:T(8,128)(2,1)S(1)}, u32[]{:S(2)}, u32[]{:S(2)}) collective-permute-start(bf16[512,896]{1,0:T(8,128)(2,1)S(1)} %bitcast.198), channel_id=1, source_target_pairs={{0,16},{8,24},{16,0},{24,8},{1,17},{9,25},{17,1},{25,9},{2,18},{10... | collective-permute-start | bytes 2752520 | tf_op jit(solution)/shard_map/ppermute | solution.py:105
  293.1 20.7 %collective-permute-start.5 = (bf16[1024,896]{1,0:T(8,128)(2,1)S(1)}, bf16[1024,896]{1,0:T(8,128)(2,1)}, u32[]{:S(2)}, u32[]{:S(2)}) collective-permute-start(bf16[1024,896]{1,0:T(8,128)(2,1)S(1)} %pad_maximum_fusion.6), channel_id=1, source_target_pairs={{0,8},{8,0},{16,24},{24,16},{1,9},{9,1},{17,25},{25,17},{2,10},{10... | collective-permute-start | bytes 5505032 | tf_op jit(solution)/shard_map/ppermute | solution.py:105
  344.1 35.9 %collective-permute-start.2 = (bf16[1024,896]{1,0:T(8,128)(2,1)}, bf16[1024,896]{1,0:T(8,128)(2,1)}, u32[]{:S(2)}, u32[]{:S(2)}) collective-permute-start(bf16[1024,896]{1,0:T(8,128)(2,1)} %slice.236), channel_id=1, source_target_pairs={{0,8},{8,0},{16,24},{24,16},{1,9},{9,1},{17,25},{25,17},{2,10},{10... | collective-permute-start | bytes 5505032 | tf_op jit(solution)/shard_map/ppermute | solution.py:105
  363.0 20.6 %collective-permute-start.6 = (bf16[1024,896]{1,0:T(8,128)(2,1)}, bf16[1024,896]{1,0:T(8,128)(2,1)}, u32[]{:S(2)}, u32[]{:S(2)}) collective-permute-start(bf16[1024,896]{1,0:T(8,128)(2,1)} %slice.240), channel_id=1, source_target_pairs={{0,8},{8,0},{16,24},{24,16},{1,9},{9,1},{17,25},{25,17},{2,10},{10... | collective-permute-start | bytes 5505032 | tf_op jit(solution)/shard_map/ppermute | solution.py:105
  382.1 43.7 %collective-permute-start.3 = (bf16[512,896]{1,0:T(8,128)(2,1)S(1)}, bf16[512,896]{1,0:T(8,128)(2,1)S(1)}, u32[]{:S(2)}, u32[]{:S(2)}) collective-permute-start(bf16[512,896]{1,0:T(8,128)(2,1)S(1)} %slice.309), channel_id=1, source_target_pairs={{0,16},{8,24},{16,0},{24,8},{1,17},{9,25},{17,1},{25,9},{2,18},{10... | collective-permute-start | bytes 2752520 | tf_op jit(solution)/shard_map/ppermute | solution.py:105
  385.6 38.9 %collective-permute-start.7 = (bf16[512,896]{1,0:T(8,128)(2,1)S(1)}, bf16[512,896]{1,0:T(8,128)(2,1)S(1)}, u32[]{:S(2)}, u32[]{:S(2)}) collective-permute-start(bf16[512,896]{1,0:T(8,128)(2,1)S(1)} %slice.308), channel_id=1, source_target_pairs={{0,16},{8,24},{16,0},{24,8},{1,17},{9,25},{17,1},{25,9},{2,18},{10... | collective-permute-start | bytes 2752520 | tf_op jit(solution)/shard_map/ppermute | solution.py:105
  456.0 194.3 %reduce-scatter.15.cloned.1.call-start = ((), (), s32[]{:S(2)}) async-start(), calls=%async_computation.10 | async-start | bytes 2451456
  460.6 261.4 %reduce-scatter.11.cloned.1.call-start = ((), (), s32[]{:S(2)}) async-start(), calls=%async_computation.7 | async-start | bytes 2359296 | tf_op jit(solution)/shard_map/reduce_scatter | solution.py:347
  590.6 59.9 %copy-start.40 = (f32[1,2,2,128]{3,2,1,0:T(2,128)S(1)}, f32[1,2,2,128]{3,2,1,0:T(2,128)}, u32[]{:S(2)}) copy-start(f32[1,2,2,128]{3,2,1,0:T(2,128)} %get-tuple-element.186) | copy-start | bytes 6148
  590.6 59.9 %copy-start.38 = (bf16[896]{0:T(1024)(128)(2,1)S(1)}, bf16[896]{0:T(1024)(128)(2,1)}, u32[]{:S(2)}) copy-start(bf16[896]{0:T(1024)(128)(2,1)} %get-tuple-element.139) | copy-start | bytes 5380
  590.6 60.0 %copy-start.6 = (bf16[2,2048,128]{1,2,0:T(8,128)(2,1)S(1)}, bf16[2,2048,128]{1,2,0:T(8,128)(2,1)}, u32[]{:S(2)}) copy-start(bf16[2,2048,128]{1,2,0:T(8,128)(2,1)} %copy-done.5) | copy-start | bytes 3145732
  650.4 149.3 %reduce-scatter.17.cloned.1.call-start = ((), (), s32[]{:S(2)}) async-start(), calls=%async_computation.11 | async-start | bytes 2488320
  668.6 55.3 %copy-start.11 = (bf16[2,256,896]{2,1,0:T(8,128)(2,1)S(1)}, bf16[2,256,896]{2,1,0:T(8,128)(2,1)}, u32[]{:S(2)}) copy-start(bf16[2,256,896]{2,1,0:T(8,128)(2,1)} %param.17) | copy-start | bytes 2752516
  668.6 55.3 %copy-start.36 = (f32[896]{0:T(1024)S(1)}, f32[896]{0:T(1024)}, u32[]{:S(2)}) copy-start(f32[896]{0:T(1024)} %copy-done.35) | copy-start | bytes 10756
  732.0 3.2 collective-permute-start.10
  733.2 22.7 %collective-permute-start.12 = (bf16[1,112,2496]{2,1,0:T(8,128)(2,1)}, bf16[1,112,2496]{2,1,0:T(8,128)(2,1)}, u32[]{:S(2)}, u32[]{:S(2)}) collective-permute-start(bf16[1,112,2496]{2,1,0:T(8,128)(2,1)} %copy.124), channel_id=1, source_target_pairs={{0,16},{8,24},{16,0},{24,8},{1,17},{9,25},{17,1},{25,9},{2,18},{10... | collective-permute-start | bytes 1677320 | tf_op jit(solution)/shard_map/ppermute | solution.py:105
  734.6 20.4 %collective-permute-start.14 = (bf16[1,152,896]{2,1,0:T(8,128)(2,1)S(1)}, bf16[1,152,896]{2,1,0:T(8,128)(2,1)S(1)}, u32[]{:S(2)}, u32[]{:S(2)}) collective-permute-start(bf16[1,152,896]{2,1,0:T(8,128)(2,1)S(1)} %bitcast.215), channel_id=1, source_target_pairs={{0,16},{8,24},{16,0},{24,8},{1,17},{9,25},{17,1},{25,9},{2,18},{10... | collective-permute-start | bytes 817160 | tf_op jit(solution)/shard_map/ppermute | solution.py:105
  736.2 34.0 %collective-permute-start.11 = (bf16[112,896]{0,1:T(8,128)(2,1)S(1)}, bf16[112,896]{0,1:T(8,128)(2,1)}, u32[]{:S(2)}, u32[]{:S(2)}) collective-permute-start(bf16[112,896]{0,1:T(8,128)(2,1)S(1)} %add_convert_fusion.4), channel_id=1, source_target_pairs={{0,16},{8,24},{16,0},{24,8},{1,17},{9,25},{17,1},{25,9},{2,18},{10... | collective-permute-start | bytes 602120 | tf_op jit(solution)/shard_map/ppermute | solution.py:105
  755.8 16.4 %collective-permute-start.15 = (bf16[2,152,896]{2,1,0:T(8,128)(2,1)}, bf16[2,152,896]{2,1,0:T(8,128)(2,1)}, u32[]{:S(2)}, u32[]{:S(2)}) collective-permute-start(bf16[2,152,896]{2,1,0:T(8,128)(2,1)} %pad_maximum_fusion.19), channel_id=1, source_target_pairs={{0,8},{8,0},{16,24},{24,16},{1,9},{9,1},{17,25},{25,17},{2,10},{10... | collective-permute-start | bytes 1634312 | tf_op jit(solution)/shard_map/ppermute | solution.py:105
  761.3 14.1 %collective-permute-start.13 = (bf16[2,112,2496]{2,1,0:T(8,128)(2,1)}, bf16[2,112,2496]{2,1,0:T(8,128)(2,1)}, u32[]{:S(2)}, u32[]{:S(2)}) collective-permute-start(bf16[2,112,2496]{2,1,0:T(8,128)(2,1)} %copy.126), channel_id=1, source_target_pairs={{0,8},{8,0},{16,24},{24,16},{1,9},{9,1},{17,25},{25,17},{2,10},{10... | collective-permute-start | bytes 3354632 | tf_op jit(solution)/shard_map/ppermute | solution.py:105
  799.7 13.8 %collective-permute-start.8 = (bf16[120,1152]{1,0:T(8,128)(2,1)}, bf16[120,1152]{1,0:T(8,128)(2,1)S(1)}, u32[]{:S(2)}, u32[]{:S(2)}) collective-permute-start(bf16[120,1152]{1,0:T(8,128)(2,1)} %bitcast.231), channel_id=1, source_target_pairs={{0,8},{8,0},{16,24},{24,16},{1,9},{9,1},{17,25},{25,17},{2,10},{10... | collective-permute-start | bytes 829448 | tf_op jit(solution)/shard_map/ppermute | solution.py:105
  813.7 8.1 collective-permute-start.9
  (41 other events, 339.5 us)
Sparse Core Ops, SparseCore 0:
  13.3 53.2 all-gather.11
  82.1 61.2 all-gather.5
  146.1 96.0 all-gather.7
  248.1 47.5 all-gather.9
  456.2 116.4 reduce-scatter.12
  576.6 73.7 reduce-scatter.14
  654.9 67.1 reduce-scatter.10
  732.1 67.6 reduce-scatter.16
